TPU v7x, 32 devices: a whole 2x2x4 slice. The times are simulated.
32 devices in a mesh: storey: 8 (over z, x), plate: 4 (over y, core).
Axes of the slice: x: 2, y: 2, z: 4, core: 2. Of those that a mesh axis runs over, the one named last changes fastest.
Arguments:
- load: float32 [1024, 2048], P('storey', 'plate'), may hold values from -6 to 6
- disp: float32 [1024, 2048], P('storey', 'plate'), may hold values from -2 to 2
- mass: float32 [1024, 2048], P('storey', 'plate'), may hold values from 0.05 to 0.5
- wall_class: int32 [1024, 2048], P('storey', 'plate'), may hold values from 0 to 3
- class_stiff: float32 [4], replicated, may hold values from 0.5 to 2
- damper_map: int32 [1024, 2048], P('storey', 'plate'), may hold values from 0 to 63
- damper_coef: float32 [512], P('storey'), may hold values from 0.2 to 2
- band_tile: float32 [4096, 2048], P('storey', 'plate')
- panel_store: float32 [1024, 512], P('storey', 'plate')
- owner: int32 [8], P('storey'), may hold values from 0 to 3
- node_index: int32 [8, 128], P('storey', 'plate'), may hold values from 0 to 65535, as said below
Outputs:
- new_disp: float32 [1024, 2048], P('storey', 'plate')
- adjoint: float32 [1024, 2048], P('storey', 'plate')
- shear: float32 [1024], P('storey')
- grads: float32 [512], P('storey')
Inputs may be any that keep to these rules, and one draw needn't show every extreme that they name: `node_index`: the 32 nodes of one plate block of a group lie in distinct rows of the block, each given as row * 512 + column within the block.
All inputs are finite; a program needn't handle non-finite values.
Results may differ from a plain program's by a relative error of at most 0.0003.
Values sent between devices are 32-bit elements; how exact they have to be, the bound alone decides.
A program may use at most 64 MiB of HBM per device.

v0:
```python
import math

import jax
import jax.numpy as jnp
from jax import lax
from jax.sharding import PartitionSpec as P

ITERS = 6


KF = 5.0 / 9.0
CM = 2.16
CD = 1.1
HIGH = lax.Precision.HIGHEST


def with_halo(x, sides, width):
    for axis, dim in sides:
        devices, length = (lax.axis_size(axis), x.shape[dim])
        up = [(i, (i + 1) % devices) for i in range(devices - 1)]
        down = [(j, i) for i, j in up]
        last = lax.slice_in_dim(x, length - width, length, axis=dim)
        first = lax.slice_in_dim(x, 0, width, axis=dim)
        before = lax.ppermute(last, axis, up)
        after = lax.ppermute(first, axis, down)
        x = jnp.concatenate([before, x, after], axis=dim)
    return x


def from_root(value, axis, source):
    kept = jnp.where(lax.axis_index(axis) == source, value, 0).astype(value.dtype)
    return lax.psum(kept, axis)


def neighbours(field):
    padded = with_halo(field, (("storey", 0), ("plate", 1)), 1)
    return padded[2:, 1:-1] + padded[:-2, 1:-1] + padded[1:-1, 2:] + padded[1:-1, :-2]


def group_totals(value):
    return lax.all_gather(value[None], "storey", axis=0, tiled=True)


def damper_lookup(ids, coef):
    rows, cols = ids.shape
    blocks = ids.reshape(rows // 16, 16, cols)
    labels = jnp.arange(coef.shape[0], dtype=jnp.int32)

    def one_block(block):
        match = block[None, :, :] == labels[:, None, None]
        return jnp.sum(jnp.where(match, coef[:, None, None], 0.0), axis=0)

    return lax.map(one_block, blocks).reshape(rows, cols)


def damper_totals(ids, values, count):
    rows, cols = ids.shape
    labels = jnp.arange(count, dtype=jnp.int32)

    def one_block(pair):
        match = pair[0][None, :, :] == labels[:, None, None]
        return jnp.sum(jnp.where(match, pair[1][None, :, :], 0.0), axis=(1, 2))

    parts = lax.map(
        one_block, (ids.reshape(rows // 16, 16, cols), values.reshape(rows // 16, 16, cols))
    )
    return jnp.sum(parts, axis=0)


def on_device(
    load,
    disp,
    mass,
    wall_class,
    class_stiff,
    damper_map,
    damper_coef,
    band_tile,
    panel_store,
    owner,
    node_index,
):
    rows, cols = load.shape
    n_storey = lax.axis_size("storey")
    n_plate = lax.axis_size("plate")
    total_rows = rows * n_storey
    total_cols = cols * n_plate
    nodes = node_index.shape[1]
    stiff = jnp.zeros_like(load)
    for level in range(class_stiff.shape[0]):
        stiff = stiff + jnp.where(wall_class == level, class_stiff[level], 0.0)
    stiff = KF * stiff
    inertia = CM * mass
    damping = CD * damper_lookup(damper_map, damper_coef)
    diag = 4.0 * stiff + inertia + damping
    root = owner[0]
    places = node_index[0]
    here_plate = lax.axis_index("plate")
    panel_use = from_root(panel_store, "plate", root)

    def correct(resid, transpose):
        scaled = resid / diag
        if transpose:
            result = lax.dot_general(scaled, band_tile, (((1,), (1,)), ((), ())), precision=HIGH)
        else:
            result = jnp.dot(scaled, band_tile, precision=HIGH)
        picked = resid.reshape(-1)[places]
        values = lax.all_gather(picked, "plate", axis=0, tiled=True)
        if transpose:
            local_coarse = jnp.dot(values, panel_use, precision=HIGH)
        else:
            local_coarse = jnp.dot(panel_use, values, precision=HIGH)
        mine = lax.dynamic_slice_in_dim(local_coarse, here_plate * nodes, nodes)
        return result.reshape(-1).at[places].add(mine).reshape(rows, cols)

    new_disp = disp
    resid = load - (diag * new_disp - stiff * neighbours(new_disp))
    for step in range(ITERS):
        new_disp = new_disp + correct(resid, False)
        if step < ITERS - 1:
            resid = load - (diag * new_disp - stiff * neighbours(new_disp))
    partial_force = jnp.sum(inertia * new_disp, axis=1)
    force = lax.psum(partial_force, "plate") * (8.0 / math.sqrt(total_cols * total_rows))
    local_shear = jnp.cumsum(force[::-1])[::-1]
    order = jnp.arange(n_storey, dtype=jnp.int32)
    here = lax.axis_index("storey")
    force_totals = group_totals(jnp.sum(force))
    shear = local_shear + jnp.sum(jnp.where(order > here, force_totals, 0.0))
    shear_totals = group_totals(jnp.sum(shear))
    below = jnp.sum(jnp.where(order < here, shear_totals, 0.0))
    drift = (jnp.cumsum(shear) + below) / total_rows
    target = inertia * drift[:, None]
    adjoint = jnp.zeros_like(load)
    resid = target
    for step in range(ITERS):
        adjoint = adjoint + correct(resid, True)
        if step < ITERS - 1:
            resid = target - (diag * adjoint - neighbours(stiff * adjoint))
    partial_sums = damper_totals(damper_map, adjoint * new_disp, damper_coef.shape[0])
    sums = lax.psum(partial_sums, "plate")
    grads = -CD * 64.0 / math.sqrt(rows * total_cols / damper_coef.shape[0]) * sums
    return (new_disp, adjoint, shear, grads)


def solution(mesh):
    return jax.shard_map(
        on_device,
        mesh=mesh,
        in_specs=(
            P("storey", "plate"),
            P("storey", "plate"),
            P("storey", "plate"),
            P("storey", "plate"),
            P(),
            P("storey", "plate"),
            P("storey"),
            P("storey", "plate"),
            P("storey", "plate"),
            P("storey"),
            P("storey", "plate"),
        ),
        out_specs=(P("storey", "plate"), P("storey", "plate"), P("storey"), P("storey")),
        check_vma=False,
    )
```

profile of v0, /device:TPU:0, one launch (start us, length us, event | category | flops | bytes accessed | tf_op | source)
XLA Modules:
  0.0 422.2 jit_solution(12196881105664291457)
XLA Ops:
  8.1 4.8 %collective-permute-start.1 = (f32[1,512]{1,0:T(1,128)S(1)}, f32[1,512]{1,0:T(1,128)S(1)}, u32[]{:S(2)}, u32[]{:S(2)}) collective-permute-start(f32[1,512]{1,0:T(1,128)S(1)} %get-tuple-element.154), channel_id=1, source_target_pairs={{0,4},{4,8},{8,12},{12,16},{16,20},{20,24},{24,28},{1,5},{5,9},{9,... | collective-permute-start | bytes 6152 | tf_op jit(solution)/shard_map/ppermute | solution.py:24
  17.7 13.8 %while.22 = (s32[]{:T(128)}, f32[8,16,512]{2,1,0:T(8,128)S(1)}, s32[8,16,512]{2,1,0:T(8,128)}, f32[64]{0:T(128)}, s32[]{:T(128)}) while((s32[]{:T(128)}, f32[8,16,512]{2,1,0:T(8,128)S(1)}, s32[8,16,512]{2,1,0:T(8,128)}, f32[64]{0:T(128)}, s32[]{:T(128)}) %tuple.83), condition=%wide.region_2.3_spmd.clone, body=%wide.region_0.2_spmd.clone.sunk | while | flops 1564674 | bytes 196941 | solution.py:53
  42.0 7.4 %all-reduce = f32[128]{0:T(128)S(1)} all-reduce(f32[128]{0:T(128)S(1)} %dynamic-update-slice), channel_id=2, replica_groups=mesh['storey'=8,'plate'=4] {'plate'}, use_global_device_ids=true, to_apply=%add | all-reduce | flops 128 | bytes 1024
  52.1 4.3 %collective-permute-start.5 = (f32[1,512]{1,0:T(1,128)S(1)}, f32[1,512]{1,0:T(1,128)S(1)}, u32[]{:S(2)}, u32[]{:S(2)}) collective-permute-start(f32[1,512]{1,0:T(1,128)S(1)} %get-tuple-element.152), channel_id=1, source_target_pairs={{0,4},{4,8},{8,12},{12,16},{16,20},{20,24},{24,28},{1,5},{5,9},{9,... | collective-permute-start | bytes 6152 | tf_op jit(solution)/shard_map/ppermute | solution.py:24
  57.8 4.2 collective-permute-done.4
  71.7 8.1 %all-reduce.1 = f32[128]{0:T(128)S(1)} all-reduce(f32[128]{0:T(128)S(1)} %dynamic-update-slice.1), channel_id=3, replica_groups=mesh['storey'=8,'plate'=4] {'plate'}, use_global_device_ids=true, to_apply=%add.1 | all-reduce | flops 128 | bytes 1024
  81.1 4.4 %collective-permute-start.9 = (f32[1,512]{1,0:T(1,128)S(1)}, f32[1,512]{1,0:T(1,128)S(1)}, u32[]{:S(2)}, u32[]{:S(2)}) collective-permute-start(f32[1,512]{1,0:T(1,128)S(1)} %get-tuple-element.150), channel_id=1, source_target_pairs={{0,4},{4,8},{8,12},{12,16},{16,20},{20,24},{24,28},{1,5},{5,9},{9,... | collective-permute-start | bytes 6152 | tf_op jit(solution)/shard_map/ppermute | solution.py:24
  86.9 4.2 collective-permute-done.8
  100.8 8.1 %all-reduce.2 = f32[128]{0:T(128)S(1)} all-reduce(f32[128]{0:T(128)S(1)} %dynamic-update-slice.2), channel_id=4, replica_groups=mesh['storey'=8,'plate'=4] {'plate'}, use_global_device_ids=true, to_apply=%add.2 | all-reduce | flops 128 | bytes 1024
  114.5 4.2 collective-permute-done.12
  128.5 8.1 %all-reduce.3 = f32[128]{0:T(128)S(1)} all-reduce(f32[128]{0:T(128)S(1)} %dynamic-update-slice.3), channel_id=5, replica_groups=mesh['storey'=8,'plate'=4] {'plate'}, use_global_device_ids=true, to_apply=%add.3 | all-reduce | flops 128 | bytes 1024
  137.9 4.8 %collective-permute-start.17 = (f32[1,512]{1,0:T(1,128)S(1)}, f32[1,512]{1,0:T(1,128)S(1)}, u32[]{:S(2)}, u32[]{:S(2)}) collective-permute-start(f32[1,512]{1,0:T(1,128)S(1)} %get-tuple-element.146), channel_id=1, source_target_pairs={{0,4},{4,8},{8,12},{12,16},{16,20},{20,24},{24,28},{1,5},{5,9},{9,... | collective-permute-start | bytes 6152 | tf_op jit(solution)/shard_map/ppermute | solution.py:24
  144.0 4.2 collective-permute-done.16
  158.0 8.1 %all-reduce.4 = f32[128]{0:T(128)S(1)} all-reduce(f32[128]{0:T(128)S(1)} %dynamic-update-slice.4), channel_id=6, replica_groups=mesh['storey'=8,'plate'=4] {'plate'}, use_global_device_ids=true, to_apply=%add.4 | all-reduce | flops 128 | bytes 1024
  171.6 4.2 collective-permute-done.20
  185.6 8.1 %all-reduce.5 = f32[128]{0:T(128)S(1)} all-reduce(f32[128]{0:T(128)S(1)} %dynamic-update-slice.5), channel_id=7, replica_groups=mesh['storey'=8,'plate'=4] {'plate'}, use_global_device_ids=true, to_apply=%add.5 | all-reduce | flops 128 | bytes 1024
  195.1 7.2 %psum.22 = f32[128]{0:T(128)S(1)} all-reduce(f32[128]{0:T(128)S(1)} %get-tuple-element.108), channel_id=1, replica_groups=mesh['storey'=8,'plate'=4] {'plate'}, use_global_device_ids=true, to_apply=%region_11.12 | all-reduce | flops 128 | bytes 1024 | tf_op jit(solution)/shard_map/psum | solution.py:123
  204.4 20.0 %all-reduce.6 = f32[8]{0:T(128)S(1)} all-reduce(f32[8]{0:T(128)S(1)} %dynamic-update-slice.6), channel_id=1, replica_groups=mesh['storey'=8,'plate'=4] {'storey'}, use_global_device_ids=true, to_apply=%add.6 | all-reduce | flops 8 | bytes 64
  228.3 17.1 %all-reduce.7 = f32[8]{0:T(128)S(1)} all-reduce(f32[8]{0:T(128)S(1)} %dynamic-update-slice.7), channel_id=1, replica_groups=mesh['storey'=8,'plate'=4] {'storey'}, use_global_device_ids=true, to_apply=%add.7 | all-reduce | flops 8 | bytes 64
  249.4 5.6 %all-reduce.8 = f32[128]{0:T(128)S(1)} all-reduce(f32[128]{0:T(128)S(1)} %dynamic-update-slice.8), channel_id=8, replica_groups=mesh['storey'=8,'plate'=4] {'plate'}, use_global_device_ids=true, to_apply=%add.8 | all-reduce | flops 128 | bytes 1024
  264.1 4.2 collective-permute-done.24
  276.0 6.6 %all-reduce.9 = f32[128]{0:T(128)S(1)} all-reduce(f32[128]{0:T(128)S(1)} %dynamic-update-slice.9), channel_id=9, replica_groups=mesh['storey'=8,'plate'=4] {'plate'}, use_global_device_ids=true, to_apply=%add.9 | all-reduce | flops 128 | bytes 1024
  290.6 4.2 collective-permute-done.28
  302.5 8.3 %all-reduce.10 = f32[128]{0:T(128)S(1)} all-reduce(f32[128]{0:T(128)S(1)} %dynamic-update-slice.10), channel_id=10, replica_groups=mesh['storey'=8,'plate'=4] {'plate'}, use_global_device_ids=true, to_apply=%add.10 | all-reduce | flops 128 | bytes 1024
  318.7 4.2 collective-permute-done.32
  330.6 8.1 %all-reduce.11 = f32[128]{0:T(128)S(1)} all-reduce(f32[128]{0:T(128)S(1)} %dynamic-update-slice.11), channel_id=11, replica_groups=mesh['storey'=8,'plate'=4] {'plate'}, use_global_device_ids=true, to_apply=%add.11 | all-reduce | flops 128 | bytes 1024
  346.7 4.2 collective-permute-done.36
  358.6 8.1 %all-reduce.12 = f32[128]{0:T(128)S(1)} all-reduce(f32[128]{0:T(128)S(1)} %dynamic-update-slice.12), channel_id=12, replica_groups=mesh['storey'=8,'plate'=4] {'plate'}, use_global_device_ids=true, to_apply=%add.12 | all-reduce | flops 128 | bytes 1024
  374.6 4.2 collective-permute-done.40
  386.6 8.1 %all-reduce.13 = f32[128]{0:T(128)S(1)} all-reduce(f32[128]{0:T(128)S(1)} %dynamic-update-slice.13), channel_id=13, replica_groups=mesh['storey'=8,'plate'=4] {'plate'}, use_global_device_ids=true, to_apply=%add.13 | all-reduce | flops 128 | bytes 1024
  396.6 11.0 %while.23 = (s32[]{:T(128)}, f32[8,64]{1,0:T(8,128)S(1)}, s32[8,16,512]{2,1,0:T(8,128)}, f32[8,16,512]{2,1,0:T(8,128)S(1)}, s32[]{:T(128)}, /*index=5*/s32[]{:T(128)}) while((s32[]{:T(128)}, f32[8,64]{1,0:T(8,128)S(1)}, s32[8,16,512]{2,1,0:T(8,128)}, f32[8,16,512]{2,1,0:T(8,128)S(1)}, s32[]{:T(128)}, /*index=5*/s32[]{:T(128)}) %tuple.84), condition=%wide.region_26.27_spmd.clone, body=%wide.region_24.26_spmd.clone.sunk | while | flops 1572802 | bytes 197465 | solution.py:64
  407.6 7.2 %psum.23 = f32[64]{0:T(128)S(1)} all-reduce(f32[64]{0:T(128)S(1)} %reduce_sum.77), channel_id=1, replica_groups=mesh['storey'=8,'plate'=4] {'plate'}, use_global_device_ids=true, to_apply=%region_28.29 | all-reduce | flops 64 | bytes 512 | tf_op jit(solution)/shard_map/psum | solution.py:140
  (347 shorter events, 200.8 us)
Async XLA Ops:
  7.2 42.8 %all-reduce.16.cloned.1.call-start = ((), (), s32[]{:S(2)}) async-start(), calls=%async_computation | async-start | bytes 131072 | tf_op jit(solution)/shard_map/psum | solution.py:32
  8.1 23.5 %collective-permute-start.1 = (f32[1,512]{1,0:T(1,128)S(1)}, f32[1,512]{1,0:T(1,128)S(1)}, u32[]{:S(2)}, u32[]{:S(2)}) collective-permute-start(f32[1,512]{1,0:T(1,128)S(1)} %get-tuple-element.154), channel_id=1, source_target_pairs={{0,4},{4,8},{8,12},{12,16},{16,20},{20,24},{24,28},{1,5},{5,9},{9,... | collective-permute-start | bytes 6152 | tf_op jit(solution)/shard_map/ppermute | solution.py:24
  12.9 18.7 %collective-permute-start = (f32[1,512]{1,0:T(1,128)S(1)}, f32[1,512]{1,0:T(1,128)S(1)}, u32[]{:S(2)}, u32[]{:S(2)}) collective-permute-start(f32[1,512]{1,0:T(1,128)S(1)} %get-tuple-element.155), channel_id=1, source_target_pairs={{4,0},{8,4},{12,8},{16,12},{20,16},{24,20},{28,24},{5,1},{9,5},{13... | collective-permute-start | bytes 6152 | tf_op jit(solution)/shard_map/ppermute | solution.py:25
  31.7 5.6 %collective-permute-start.2 = (f32[130,1]{1,0:T(8,128)S(1)}, f32[130,1]{1,0:T(8,128)S(1)}, u32[]{:S(2)}, u32[]{:S(2)}) collective-permute-start(f32[130,1]{1,0:T(8,128)S(1)} %get-tuple-element.132), channel_id=1, source_target_pairs={{1,0},{2,1},{3,2},{5,4},{6,5},{7,6},{9,8},{10,9},{11,10},{13,12},{... | collective-permute-start | bytes 1568 | tf_op jit(solution)/shard_map/ppermute | solution.py:25
  33.0 4.3 %collective-permute-start.3 = (f32[130,1]{1,0:T(8,128)S(1)}, f32[130,1]{1,0:T(8,128)S(1)}, u32[]{:S(2)}, u32[]{:S(2)}) collective-permute-start(f32[130,1]{1,0:T(8,128)S(1)} %get-tuple-element.133), channel_id=1, source_target_pairs={{0,1},{1,2},{2,3},{4,5},{5,6},{6,7},{8,9},{9,10},{10,11},{12,13},{... | collective-permute-start | bytes 1568 | tf_op jit(solution)/shard_map/ppermute | solution.py:24
  52.1 5.7 %collective-permute-start.5 = (f32[1,512]{1,0:T(1,128)S(1)}, f32[1,512]{1,0:T(1,128)S(1)}, u32[]{:S(2)}, u32[]{:S(2)}) collective-permute-start(f32[1,512]{1,0:T(1,128)S(1)} %get-tuple-element.152), channel_id=1, source_target_pairs={{0,4},{4,8},{8,12},{12,16},{16,20},{20,24},{24,28},{1,5},{5,9},{9,... | collective-permute-start | bytes 6152 | tf_op jit(solution)/shard_map/ppermute | solution.py:24
  56.5 5.5 %collective-permute-start.4 = (f32[1,512]{1,0:T(1,128)S(1)}, f32[1,512]{1,0:T(1,128)S(1)}, u32[]{:S(2)}, u32[]{:S(2)}) collective-permute-start(f32[1,512]{1,0:T(1,128)S(1)} %get-tuple-element.153), channel_id=1, source_target_pairs={{4,0},{8,4},{12,8},{16,12},{20,16},{24,20},{28,24},{5,1},{9,5},{13... | collective-permute-start | bytes 6152 | tf_op jit(solution)/shard_map/ppermute | solution.py:25
  62.0 4.3 %collective-permute-start.6 = (f32[130,1]{1,0:T(8,128)S(1)}, f32[130,1]{1,0:T(8,128)S(1)}, u32[]{:S(2)}, u32[]{:S(2)}) collective-permute-start(f32[130,1]{1,0:T(8,128)S(1)} %get-tuple-element.130), channel_id=1, source_target_pairs={{1,0},{2,1},{3,2},{5,4},{6,5},{7,6},{9,8},{10,9},{11,10},{13,12},{... | collective-permute-start | bytes 1568 | tf_op jit(solution)/shard_map/ppermute | solution.py:25
  81.1 5.7 %collective-permute-start.9 = (f32[1,512]{1,0:T(1,128)S(1)}, f32[1,512]{1,0:T(1,128)S(1)}, u32[]{:S(2)}, u32[]{:S(2)}) collective-permute-start(f32[1,512]{1,0:T(1,128)S(1)} %get-tuple-element.150), channel_id=1, source_target_pairs={{0,4},{4,8},{8,12},{12,16},{16,20},{20,24},{24,28},{1,5},{5,9},{9,... | collective-permute-start | bytes 6152 | tf_op jit(solution)/shard_map/ppermute | solution.py:24
  85.6 5.5 %collective-permute-start.8 = (f32[1,512]{1,0:T(1,128)S(1)}, f32[1,512]{1,0:T(1,128)S(1)}, u32[]{:S(2)}, u32[]{:S(2)}) collective-permute-start(f32[1,512]{1,0:T(1,128)S(1)} %get-tuple-element.151), channel_id=1, source_target_pairs={{4,0},{8,4},{12,8},{16,12},{20,16},{24,20},{28,24},{5,1},{9,5},{13... | collective-permute-start | bytes 6152 | tf_op jit(solution)/shard_map/ppermute | solution.py:25
  91.1 4.3 %collective-permute-start.10 = (f32[130,1]{1,0:T(8,128)S(1)}, f32[130,1]{1,0:T(8,128)S(1)}, u32[]{:S(2)}, u32[]{:S(2)}) collective-permute-start(f32[130,1]{1,0:T(8,128)S(1)} %get-tuple-element.128), channel_id=1, source_target_pairs={{1,0},{2,1},{3,2},{5,4},{6,5},{7,6},{9,8},{10,9},{11,10},{13,12},{... | collective-permute-start | bytes 1568 | tf_op jit(solution)/shard_map/ppermute | solution.py:25
  110.2 4.3 %collective-permute-start.13 = (f32[1,512]{1,0:T(1,128)S(1)}, f32[1,512]{1,0:T(1,128)S(1)}, u32[]{:S(2)}, u32[]{:S(2)}) collective-permute-start(f32[1,512]{1,0:T(1,128)S(1)} %get-tuple-element.148), channel_id=1, source_target_pairs={{0,4},{4,8},{8,12},{12,16},{16,20},{20,24},{24,28},{1,5},{5,9},{9,... | collective-permute-start | bytes 6152 | tf_op jit(solution)/shard_map/ppermute | solution.py:24
  113.2 5.5 %collective-permute-start.12 = (f32[1,512]{1,0:T(1,128)S(1)}, f32[1,512]{1,0:T(1,128)S(1)}, u32[]{:S(2)}, u32[]{:S(2)}) collective-permute-start(f32[1,512]{1,0:T(1,128)S(1)} %get-tuple-element.149), channel_id=1, source_target_pairs={{4,0},{8,4},{12,8},{16,12},{20,16},{24,20},{28,24},{5,1},{9,5},{13... | collective-permute-start | bytes 6152 | tf_op jit(solution)/shard_map/ppermute | solution.py:25
  118.8 4.3 %collective-permute-start.14 = (f32[130,1]{1,0:T(8,128)S(1)}, f32[130,1]{1,0:T(8,128)S(1)}, u32[]{:S(2)}, u32[]{:S(2)}) collective-permute-start(f32[130,1]{1,0:T(8,128)S(1)} %get-tuple-element.126), channel_id=1, source_target_pairs={{1,0},{2,1},{3,2},{5,4},{6,5},{7,6},{9,8},{10,9},{11,10},{13,12},{... | collective-permute-start | bytes 1568 | tf_op jit(solution)/shard_map/ppermute | solution.py:25
  137.9 6.1 %collective-permute-start.17 = (f32[1,512]{1,0:T(1,128)S(1)}, f32[1,512]{1,0:T(1,128)S(1)}, u32[]{:S(2)}, u32[]{:S(2)}) collective-permute-start(f32[1,512]{1,0:T(1,128)S(1)} %get-tuple-element.146), channel_id=1, source_target_pairs={{0,4},{4,8},{8,12},{12,16},{16,20},{20,24},{24,28},{1,5},{5,9},{9,... | collective-permute-start | bytes 6152 | tf_op jit(solution)/shard_map/ppermute | solution.py:24
  142.7 5.5 %collective-permute-start.16 = (f32[1,512]{1,0:T(1,128)S(1)}, f32[1,512]{1,0:T(1,128)S(1)}, u32[]{:S(2)}, u32[]{:S(2)}) collective-permute-start(f32[1,512]{1,0:T(1,128)S(1)} %get-tuple-element.147), channel_id=1, source_target_pairs={{4,0},{8,4},{12,8},{16,12},{20,16},{24,20},{28,24},{5,1},{9,5},{13... | collective-permute-start | bytes 6152 | tf_op jit(solution)/shard_map/ppermute | solution.py:25
  148.3 4.5 %collective-permute-start.18 = (f32[130,1]{1,0:T(8,128)S(1)}, f32[130,1]{1,0:T(8,128)S(1)}, u32[]{:S(2)}, u32[]{:S(2)}) collective-permute-start(f32[130,1]{1,0:T(8,128)S(1)} %get-tuple-element.124), channel_id=1, source_target_pairs={{1,0},{2,1},{3,2},{5,4},{6,5},{7,6},{9,8},{10,9},{11,10},{13,12},{... | collective-permute-start | bytes 1568 | tf_op jit(solution)/shard_map/ppermute | solution.py:25
  167.4 4.2 %collective-permute-start.21 = (f32[1,512]{1,0:T(1,128)S(1)}, f32[1,512]{1,0:T(1,128)S(1)}, u32[]{:S(2)}, u32[]{:S(2)}) collective-permute-start(f32[1,512]{1,0:T(1,128)S(1)} %get-tuple-element.144), channel_id=1, source_target_pairs={{0,4},{4,8},{8,12},{12,16},{16,20},{20,24},{24,28},{1,5},{5,9},{9,... | collective-permute-start | bytes 6152 | tf_op jit(solution)/shard_map/ppermute | solution.py:24
  170.3 5.5 %collective-permute-start.20 = (f32[1,512]{1,0:T(1,128)S(1)}, f32[1,512]{1,0:T(1,128)S(1)}, u32[]{:S(2)}, u32[]{:S(2)}) collective-permute-start(f32[1,512]{1,0:T(1,128)S(1)} %get-tuple-element.145), channel_id=1, source_target_pairs={{4,0},{8,4},{12,8},{16,12},{20,16},{24,20},{28,24},{5,1},{9,5},{13... | collective-permute-start | bytes 6152 | tf_op jit(solution)/shard_map/ppermute | solution.py:25
  175.9 4.9 %collective-permute-start.22 = (f32[130,1]{1,0:T(8,128)S(1)}, f32[130,1]{1,0:T(8,128)S(1)}, u32[]{:S(2)}, u32[]{:S(2)}) collective-permute-start(f32[130,1]{1,0:T(8,128)S(1)} %get-tuple-element.122), channel_id=1, source_target_pairs={{1,0},{2,1},{3,2},{5,4},{6,5},{7,6},{9,8},{10,9},{11,10},{13,12},{... | collective-permute-start | bytes 1568 | tf_op jit(solution)/shard_map/ppermute | solution.py:25
  258.8 5.2 %collective-permute-start.25 = (f32[1,512]{1,0:T(1,128)S(1)}, f32[1,512]{1,0:T(1,128)S(1)}, u32[]{:S(2)}, u32[]{:S(2)}) collective-permute-start(f32[1,512]{1,0:T(1,128)S(1)} %get-tuple-element.142), channel_id=1, source_target_pairs={{0,4},{4,8},{8,12},{12,16},{16,20},{20,24},{24,28},{1,5},{5,9},{9,... | collective-permute-start | bytes 6152 | tf_op jit(solution)/shard_map/ppermute | solution.py:24
  262.8 5.5 %collective-permute-start.24 = (f32[1,512]{1,0:T(1,128)S(1)}, f32[1,512]{1,0:T(1,128)S(1)}, u32[]{:S(2)}, u32[]{:S(2)}) collective-permute-start(f32[1,512]{1,0:T(1,128)S(1)} %get-tuple-element.143), channel_id=1, source_target_pairs={{4,0},{8,4},{12,8},{16,12},{20,16},{24,20},{28,24},{5,1},{9,5},{13... | collective-permute-start | bytes 6152 | tf_op jit(solution)/shard_map/ppermute | solution.py:25
  268.3 4.3 %collective-permute-start.26 = (f32[130,1]{1,0:T(8,128)S(1)}, f32[130,1]{1,0:T(8,128)S(1)}, u32[]{:S(2)}, u32[]{:S(2)}) collective-permute-start(f32[130,1]{1,0:T(8,128)S(1)} %get-tuple-element.120), channel_id=1, source_target_pairs={{1,0},{2,1},{3,2},{5,4},{6,5},{7,6},{9,8},{10,9},{11,10},{13,12},{... | collective-permute-start | bytes 1568 | tf_op jit(solution)/shard_map/ppermute | solution.py:25
  289.2 5.5 %collective-permute-start.28 = (f32[1,512]{1,0:T(1,128)S(1)}, f32[1,512]{1,0:T(1,128)S(1)}, u32[]{:S(2)}, u32[]{:S(2)}) collective-permute-start(f32[1,512]{1,0:T(1,128)S(1)} %get-tuple-element.141), channel_id=1, source_target_pairs={{4,0},{8,4},{12,8},{16,12},{20,16},{24,20},{28,24},{5,1},{9,5},{13... | collective-permute-start | bytes 6152 | tf_op jit(solution)/shard_map/ppermute | solution.py:25
  294.8 4.3 %collective-permute-start.30 = (f32[130,1]{1,0:T(8,128)S(1)}, f32[130,1]{1,0:T(8,128)S(1)}, u32[]{:S(2)}, u32[]{:S(2)}) collective-permute-start(f32[130,1]{1,0:T(8,128)S(1)} %get-tuple-element.118), channel_id=1, source_target_pairs={{1,0},{2,1},{3,2},{5,4},{6,5},{7,6},{9,8},{10,9},{11,10},{13,12},{... | collective-permute-start | bytes 1568 | tf_op jit(solution)/shard_map/ppermute | solution.py:25
  317.4 5.5 %collective-permute-start.32 = (f32[1,512]{1,0:T(1,128)S(1)}, f32[1,512]{1,0:T(1,128)S(1)}, u32[]{:S(2)}, u32[]{:S(2)}) collective-permute-start(f32[1,512]{1,0:T(1,128)S(1)} %get-tuple-element.139), channel_id=1, source_target_pairs={{4,0},{8,4},{12,8},{16,12},{20,16},{24,20},{28,24},{5,1},{9,5},{13... | collective-permute-start | bytes 6152 | tf_op jit(solution)/shard_map/ppermute | solution.py:25
  323.0 4.3 %collective-permute-start.34 = (f32[130,1]{1,0:T(8,128)S(1)}, f32[130,1]{1,0:T(8,128)S(1)}, u32[]{:S(2)}, u32[]{:S(2)}) collective-permute-start(f32[130,1]{1,0:T(8,128)S(1)} %get-tuple-element.116), channel_id=1, source_target_pairs={{1,0},{2,1},{3,2},{5,4},{6,5},{7,6},{9,8},{10,9},{11,10},{13,12},{... | collective-permute-start | bytes 1568 | tf_op jit(solution)/shard_map/ppermute | solution.py:25
  342.5 4.1 collective-permute-start.37
  345.3 5.5 %collective-permute-start.36 = (f32[1,512]{1,0:T(1,128)S(1)}, f32[1,512]{1,0:T(1,128)S(1)}, u32[]{:S(2)}, u32[]{:S(2)}) collective-permute-start(f32[1,512]{1,0:T(1,128)S(1)} %get-tuple-element.137), channel_id=1, source_target_pairs={{4,0},{8,4},{12,8},{16,12},{20,16},{24,20},{28,24},{5,1},{9,5},{13... | collective-permute-start | bytes 6152 | tf_op jit(solution)/shard_map/ppermute | solution.py:25
  350.9 4.3 %collective-permute-start.38 = (f32[130,1]{1,0:T(8,128)S(1)}, f32[130,1]{1,0:T(8,128)S(1)}, u32[]{:S(2)}, u32[]{:S(2)}) collective-permute-start(f32[130,1]{1,0:T(8,128)S(1)} %get-tuple-element.114), channel_id=1, source_target_pairs={{1,0},{2,1},{3,2},{5,4},{6,5},{7,6},{9,8},{10,9},{11,10},{13,12},{... | collective-permute-start | bytes 1568 | tf_op jit(solution)/shard_map/ppermute | solution.py:25
  373.3 5.5 %collective-permute-start.40 = (f32[1,512]{1,0:T(1,128)S(1)}, f32[1,512]{1,0:T(1,128)S(1)}, u32[]{:S(2)}, u32[]{:S(2)}) collective-permute-start(f32[1,512]{1,0:T(1,128)S(1)} %get-tuple-element.135), channel_id=1, source_target_pairs={{4,0},{8,4},{12,8},{16,12},{20,16},{24,20},{28,24},{5,1},{9,5},{13... | collective-permute-start | bytes 6152 | tf_op jit(solution)/shard_map/ppermute | solution.py:25
  378.9 4.4 %collective-permute-start.42 = (f32[130,1]{1,0:T(8,128)S(1)}, f32[130,1]{1,0:T(8,128)S(1)}, u32[]{:S(2)}, u32[]{:S(2)}) collective-permute-start(f32[130,1]{1,0:T(8,128)S(1)} %get-tuple-element.112), channel_id=1, source_target_pairs={{1,0},{2,1},{3,2},{5,4},{6,5},{7,6},{9,8},{10,9},{11,10},{13,12},{... | collective-permute-start | bytes 1568 | tf_op jit(solution)/shard_map/ppermute | solution.py:25
  (23 other events, 440.1 us)
Sparse Core Ops, SparseCore 0:
  15.7 34.2 all-reduce.15
where the time goes:
time: 426 us; the launch traced here: 422 us
  blocking collectives  144 us (34%)
  starting transfers between devices  102 us (24%)
  other arithmetic  61 us (14%)
  waiting for transfers between devices  50.3 us (12%)
  local copies, waits for them, and re-layouts  34 us (8%)
  between operations  16.9 us (4%)
  matrix products  14.1 us (3%)
    unnamed x14, blocking collectives  130 us
    ppermute x22, starting transfers between devices, with_halo(): before = lax.ppermute(last, axis, up)  73 us
    ppermute x22, waiting for transfers between devices, with_halo(): after = lax.ppermute(first, axis, down)  41.7 us
    ppermute x22, starting transfers between devices, with_halo(): after = lax.ppermute(first, axis, down)  28.4 us
    sub x6, other arithmetic, on_device(): resid = load - (diag * new_disp - stiff * neighbours(new_disp))  16.2 us
    mul x5, other arithmetic, on_device(): resid = target - (diag * adjoint - neighbours(stiff * adjoint))  12.8 us
    scatter-add x12, other arithmetic, correct(): return result.reshape(-1).at[places].add(mine).reshape(rows, cols)  10.5 us
    unnamed x74, local copies, waits for them, and re-layouts  8.59 us
  transfers between devices with their start and end apart: 45, of which 21 were waited for; matrix products, arithmetic and copies ran while one was open for 5% of the time, Pallas kernels for 0%

commit v1 on v0

v1 whole, which is shorter than its diff:
```python
import functools
import math

import jax
import jax.numpy as jnp
from jax import lax
from jax.experimental import pallas as pl
from jax.experimental.pallas import tpu as pltpu
from jax.sharding import PartitionSpec as P

ITERS = 6
KF = 5.0 / 9.0
CM = 2.16
CD = 1.1
HIGH = lax.Precision.HIGHEST
MESH = pl.DeviceIdType.MESH
F32 = jnp.float32
BF16 = jnp.bfloat16
LANES = 128


def iota(shape, dim):
    return lax.broadcasted_iota(jnp.int32, shape, dim)


def to_row(col):
    n = col.shape[0]
    return jnp.sum(jnp.where(iota((n, n), 0) == iota((n, n), 1), col, 0.0), axis=0, keepdims=True)


def to_col(row):
    n = row.shape[1]
    return jnp.sum(jnp.where(iota((n, n), 0) == iota((n, n), 1), row, 0.0), axis=1, keepdims=True)


def split(value):
    hi = value.astype(BF16)
    return hi, (value - hi.astype(F32)).astype(BF16)


def wait_bytes(ref, sem):
    pltpu.make_async_copy(ref, ref, sem).wait()


def kernel(
    ns, np_,
    load, disp, mass, wall, cstiff, dmap, coef, tile, panel, owner, nidx,
    out_disp, out_adj, out_shear, out_grads,
    stiff, diag, rdiag, cm, place, x, r, q, z,
    t_hi, t_lo, tt_hi, tt_lo,
    pan_own, pan_left, pan_right, info_out, info_in,
    spk, sslots, snb, pslots,
    pk, slots, nbs,
    apk, fslots, tslots, gslots, seg,
    s_send, s_recv, n_send, n_recv, p_send, p_recv, i_send, i_recv,
    r_send, r_recv, rn_send, rn_recv, a_send, a_recv,
):
    rows, cols = load.shape
    nodes = nidx.shape[1]
    order = nodes * np_
    count = coef.shape[0]
    width = spk.shape[1]
    pieces = cols // LANES
    s = lax.axis_index("storey")
    b = lax.axis_index("plate")
    has = (s > 0, s < ns - 1)
    beside = (s - 1, s + 1)

    barrier = pltpu.get_barrier_semaphore()
    for d in range(1, np_):
        pl.semaphore_signal(barrier, inc=1, device_id=(s, (b + d) % np_), device_id_type=MESH)
    for d in range(1, ns):
        pl.semaphore_signal(barrier, inc=1, device_id=((s + d) % ns, b), device_id_type=MESH)
    for way in range(2):
        @pl.when(has[way])
        def _():
            for d in range(1, np_):
                pl.semaphore_signal(barrier, inc=1, device_id=(beside[way], (b + d) % np_), device_id_type=MESH)
    sides = jnp.minimum(s, 1) + jnp.minimum(ns - 1 - s, 1)
    pl.semaphore_wait(barrier, np_ - 1 + ns - 1 + sides * (np_ - 1))

    def push(src, dst, send, recv, where):
        pltpu.make_async_remote_copy(
            src_ref=src, dst_ref=dst, send_sem=send, recv_sem=recv, device_id=where, device_id_type=MESH
        ).start()

    def to_plates(src, dst, send, recv):
        for d in range(1, np_):
            push(src, dst, send, recv, (s, (b + d) % np_))

    to_plates(panel, pslots.at[b], p_send, p_recv)

    level = jnp.zeros((rows, cols), F32)
    for c in range(cstiff.shape[0]):
        level = jnp.where(wall[...] == c, cstiff[c], level)
    stiff[...] = KF * level
    spk[...] = jnp.zeros(spk.shape, F32)
    spk[0:1, 0:cols] = disp[0:1, :]
    spk[1:2, 0:cols] = disp[rows - 1 : rows, :]
    tiled = (iota((nodes, order), 1) % nodes == iota((nodes, order), 0)).astype(F32)
    spk[2:3, 0:order] = jnp.dot(nidx[...].astype(F32), tiled, precision=HIGH, preferred_element_type=F32)
    spk[3:4, 0:rows] = to_row(disp[:, 0:1])
    spk[4:5, 0:rows] = to_row(disp[:, cols - 1 : cols])
    spk[5:6, 0:rows] = to_row(stiff[:, 0:1])
    spk[6:7, 0:rows] = to_row(stiff[:, cols - 1 : cols])
    to_plates(spk, sslots.at[b], s_send, s_recv)
    for way in range(2):
        @pl.when(has[way])
        def _():
            push(spk, snb.at[1 - way], n_send.at[way], n_recv.at[1 - way], (beside[way], b))

        @pl.when(jnp.logical_not(has[way]))
        def _():
            snb[way] = jnp.zeros(snb.shape[1:], F32)
            info_in[way] = jnp.zeros(info_in.shape[1:], F32)
            nbs[0, way] = jnp.zeros(nbs.shape[2:], F32)
            nbs[1, way] = jnp.zeros(nbs.shape[2:], F32)

    cm[...] = CM * mass[...]

    def lookup(i, carry):
        part = pl.ds(pl.multiple_of(i * 8, 8), 8)
        ids = dmap[part, :]
        value = jnp.zeros(ids.shape, F32)
        for d in range(count):
            value = jnp.where(ids == d, coef[d], value)
        total = 4.0 * stiff[part, :] + cm[part, :] + CD * value
        diag[part, :] = total
        rdiag[part, :] = 1.0 / total
        return carry

    lax.fori_loop(0, rows // 8, lookup, 0)
    t_hi[...], t_lo[...] = split(tile[...])
    tt_hi[...], tt_lo[...] = split(tile[...].T)

    pslots[b] = panel[...]
    sslots[b] = spk[...]
    wait_bytes(sslots.at[pl.ds(0, np_ - 1)], s_recv)
    wait_bytes(pslots.at[pl.ds(0, np_ - 1)], p_recv)
    for way in range(2):
        @pl.when(has[way])
        def _():
            wait_bytes(snb.at[way], n_recv.at[way])
            wait_bytes(spk, n_send.at[way])
    wait_bytes(sslots.at[pl.ds(0, np_ - 1)], s_send)
    wait_bytes(pslots.at[pl.ds(0, np_ - 1)], p_send)

    root = owner[0]
    used = jnp.zeros((order, order), F32)
    lane_node = iota((1, order), 1) // nodes
    where_all = jnp.zeros((1, order), F32)
    for j in range(np_):
        used = jnp.where(root == j, pslots[j], used)
        where_all = jnp.where(lane_node == j, sslots[j, 2:3, 0:order], where_all)
    at = where_all.astype(jnp.int32)
    shift = cols.bit_length() - 1
    at_row = jnp.right_shift(at, shift)
    at_col = jnp.bitwise_and(at, cols - 1)
    at_row_col = to_col(at_row.astype(F32)).astype(jnp.int32)
    wide = (order, np_ * rows)
    spread = (
        (iota(wide, 1) % rows == at_row_col) & (iota(wide, 1) // rows == iota(wide, 0) // nodes)
    ).astype(F32)
    tall = (rows, order)
    at_h = iota(tall, 0) == at_row
    pick_own = (at_h & (lane_node == b)).astype(F32)
    pick_left = (at_h & (lane_node == b - 1) & (at_col == cols - 1)).astype(F32)
    pick_right = (at_h & (lane_node == b + 1) & (at_col == 0)).astype(F32)
    col_of = jnp.sum(pick_own * (at_col + 1).astype(F32), axis=1, keepdims=True).astype(jnp.int32) - 1
    place[...] = (iota((rows, cols), 1) == col_of).astype(F32)
    left_slot = jnp.maximum(b - 1, 0)
    right_slot = jnp.minimum(b + 1, np_ - 1)
    stiff_left = to_col(sslots[left_slot][6:7, 0:rows])
    stiff_right = to_col(sslots[right_slot][5:6, 0:rows])
    stiff_own = jnp.sum(place[...] * stiff[...], axis=1, keepdims=True)
    info_out[...] = jnp.zeros(info_out.shape, F32)
    info_out[4:5, 0:cols] = place[0:1, :]
    info_out[5:6, 0:cols] = place[rows - 1 : rows, :]
    for mode in range(2):
        grown = jnp.dot(used.T if mode else used, spread, precision=HIGH, preferred_element_type=F32)
        own = jnp.dot(pick_own, grown, precision=HIGH, preferred_element_type=F32)
        left = jnp.dot(pick_left, grown, precision=HIGH, preferred_element_type=F32)
        right = jnp.dot(pick_right, grown, precision=HIGH, preferred_element_type=F32)
        pan_own[mode] = own
        pan_left[mode] = left * stiff_left if mode else left
        pan_right[mode] = right * stiff_right if mode else right
        edge = own * stiff_own if mode else own
        info_out[2 * mode : 2 * mode + 1, 0 : np_ * rows] = edge[0:1, :]
        info_out[2 * mode + 1 : 2 * mode + 2, 0 : np_ * rows] = edge[rows - 1 : rows, :]
    for way in range(2):
        @pl.when(has[way])
        def _():
            push(info_out, info_in.at[1 - way], i_send.at[way], i_recv.at[1 - way], (beside[way], b))

    eye = (iota((rows, rows), 0) == iota((rows, rows), 1)).astype(F32)
    lane = iota((rows, cols), 1)
    line = iota((rows, cols), 0)

    def neighbours(v, top, bottom, left, right):
        above = jnp.where(line == 0, top, pltpu.roll(v, 1, 0))
        below = jnp.where(line == rows - 1, bottom, pltpu.roll(v, rows - 1, 0))
        west = jnp.where(lane == 0, left, pltpu.roll(v, 1, 1))
        east = jnp.where(lane == cols - 1, right, pltpu.roll(v, cols - 1, 1))
        return above + below + west + east

    def send_round(mode, par):
        resid = r[...]
        hi, lo = split(resid * rdiag[...])
        wh, wl = (tt_hi, tt_lo) if mode else (t_hi, t_lo)
        both = jnp.dot(jnp.concatenate([hi, lo], axis=0), wh[...], preferred_element_type=F32)
        band = both[:rows] + both[rows:] + jnp.dot(hi, wl[...], preferred_element_type=F32)
        z[...] = x[...] + band
        here = pk.at[par]
        edge = (lambda *at: z[at] * stiff[at]) if mode else (lambda *at: z[at])
        first, last = edge(slice(0, 1), slice(None)), edge(slice(rows - 1, rows), slice(None))
        for t in range(pieces):
            here[1, t : t + 1, :] = first[:, t * LANES : (t + 1) * LANES]
            here[1, pieces + t : pieces + t + 1, :] = last[:, t * LANES : (t + 1) * LANES]
        here[0, 0:1, :] = to_row(jnp.sum(resid * place[...], axis=1, keepdims=True))
        here[0, 1:2, :] = to_row(edge(slice(None), slice(0, 1)))
        here[0, 2:3, :] = to_row(edge(slice(None), slice(cols - 1, cols)))
        to_plates(here.at[0], slots.at[par, b], r_send.at[par], r_recv.at[par])
        for way in range(2):
            @pl.when(has[way])
            def _():
                for d in range(np_):
                    push(
                        here.at[0], nbs.at[par, 1 - way, b], rn_send.at[par, way],
                        rn_recv.at[par, 1 - way], (beside[way], (b + d) % np_),
                    )
                push(
                    here.at[1], nbs.at[par, 1 - way, np_], rn_send.at[par, way],
                    rn_recv.at[par, 1 - way], (beside[way], b),
                )
        slots[par, b] = here[0]

    def wait_round(par):
        wait_bytes(slots.at[par, pl.ds(0, np_ - 1)], r_recv.at[par])
        wait_bytes(slots.at[par, pl.ds(0, np_ - 1)], r_send.at[par])
        for way in range(2):
            @pl.when(has[way])
            def _():
                wait_bytes(nbs.at[par, way], rn_recv.at[par, way])
                wait_bytes(nbs.at[par, way], rn_send.at[par, way])

    def applied(mat, mode, par, extra=None):
        total = extra
        for j in range(np_):
            term = mat[mode, :, j * rows : (j + 1) * rows] * slots[par, j, 0:1, :]
            total = term if total is None else total + term
        return jnp.sum(total, axis=1, keepdims=True)

    def finish(mode, par):
        x[...] = z[...] + applied(pan_own, mode, par) * place[...]

    def side_row(mode, par, way):
        pan_row = 2 * mode + (1 - way)
        total = jnp.zeros((1, rows), F32)
        for j in range(np_):
            total = total + info_in[way, pan_row : pan_row + 1, j * rows : (j + 1) * rows] * nbs[par, way, j, 0:1, :]
        value = jnp.sum(total, axis=1, keepdims=True)
        base = pieces * (1 - way)
        got = jnp.concatenate([nbs[par, way, np_, base + t : base + t + 1, :] for t in range(pieces)], axis=1)
        return got + value * info_in[way, 4 + (1 - way) : 5 + (1 - way), 0:cols]

    def halos(mode, par):
        west = jnp.where(b > 0, eye * slots[par, left_slot, 2:3, :], 0.0)
        east = jnp.where(b < np_ - 1, eye * slots[par, right_slot, 1:2, :], 0.0)
        return (
            side_row(mode, par, 0),
            side_row(mode, par, 1),
            applied(pan_left, mode, par, west),
            applied(pan_right, mode, par, east),
        )

    x[...] = disp[...]
    west = jnp.where(b > 0, to_col(sslots[left_slot][4:5, 0:rows]), 0.0)
    east = jnp.where(b < np_ - 1, to_col(sslots[right_slot][3:4, 0:rows]), 0.0)
    around = neighbours(disp[...], snb[0, 1:2, 0:cols], snb[1, 0:1, 0:cols], west, east)
    r[...] = load[...] - (diag[...] * disp[...] - stiff[...] * around)

    def primal(k, carry):
        par = lax.rem(k, 2)
        send_round(0, par)

        @pl.when(k == 0)
        def _():
            for way in range(2):
                @pl.when(has[way])
                def _():
                    wait_bytes(info_in.at[way], i_recv.at[way])
                    wait_bytes(info_out, i_send.at[way])

        wait_round(par)
        finish(0, par)
        v = x[...]
        r[...] = load[...] - (diag[...] * v - stiff[...] * neighbours(v, *halos(0, par)))
        return carry

    lax.fori_loop(0, ITERS - 1, primal, 0)
    par = (ITERS - 1) % 2
    send_round(0, par)
    wait_round(par)
    finish(0, par)
    out_disp[...] = x[...]

    apk[...] = jnp.zeros(apk.shape, F32)
    apk[0, 0:1, :] = to_row(jnp.sum(cm[...] * x[...], axis=1, keepdims=True))
    to_plates(apk.at[0], fslots.at[b], a_send.at[0], a_recv.at[0])
    fslots[b] = apk[0]
    wait_bytes(fslots.at[pl.ds(0, np_ - 1)], a_recv.at[0])
    wait_bytes(fslots.at[pl.ds(0, np_ - 1)], a_send.at[0])
    force = fslots[0, 0:1, :]
    for j in range(1, np_):
        force = force + fslots[j, 0:1, :]
    force = force * (8.0 / math.sqrt(cols * np_ * rows * ns))
    apk[1, 0:1, :] = force
    for d in range(1, ns):
        push(apk.at[1], tslots.at[s], a_send.at[1], a_recv.at[1], ((s + d) % ns, b))
    tslots[s] = apk[1]
    wait_bytes(tslots.at[pl.ds(0, ns - 1)], a_recv.at[1])
    wait_bytes(tslots.at[pl.ds(0, ns - 1)], a_send.at[1])
    over = jnp.zeros((1, rows), F32)
    under = jnp.zeros((1, rows), F32)
    weight = (iota((1, rows), 1) + 1).astype(F32)
    for j in range(ns):
        line_j = tslots[j, 0:1, :]
        over = over + jnp.where(s < j, line_j, 0.0)
        under = under + line_j * (jnp.where(s > j, weight, 0.0) + (rows * jnp.minimum(s, j)).astype(F32))
    over = jnp.sum(over, axis=1, keepdims=True)
    under = jnp.sum(under, axis=1, keepdims=True)
    hh, ll = iota((rows, rows), 0), iota((rows, rows), 1)
    shear = jnp.sum(jnp.where(ll >= hh, force, 0.0), axis=1, keepdims=True) + over
    out_shear[...] = to_row(shear)
    local = jnp.sum(force * (jnp.minimum(hh, ll) + 1).astype(F32), axis=1, keepdims=True)
    step = (iota((rows, 1), 0) + 1).astype(F32)
    drift = (local + step * over + under) * (1.0 / (rows * ns))
    q[...] = cm[...] * drift
    r[...] = q[...]
    x[...] = jnp.zeros((rows, cols), F32)

    def adjoint(k, carry):
        par = lax.rem(k, 2)
        send_round(1, par)
        wait_round(par)
        finish(1, par)
        v = x[...]
        r[...] = q[...] - (diag[...] * v - neighbours(stiff[...] * v, *halos(1, par)))
        return carry

    lax.fori_loop(0, ITERS - 1, adjoint, 0)
    send_round(1, par)
    wait_round(par)
    finish(1, par)
    out_adj[...] = x[...]

    z[...] = x[...] * out_disp[...]
    group = 8
    for first in range(0, count, group):
        def gather(i, accs):
            part = pl.ds(pl.multiple_of(i * 8, 8), 8)
            ids, vals = dmap[part, :], z[part, :]
            res = []
            for d in range(group):
                kept = jnp.where(ids == first + d, vals, 0.0)
                acc = accs[d]
                for t in range(pieces):
                    acc = acc + kept[:, t * LANES : (t + 1) * LANES]
                res.append(acc)
            return tuple(res)

        accs = lax.fori_loop(0, rows // 8, gather, tuple(jnp.zeros((8, LANES), F32) for _ in range(group)))
        for d in range(group):
            seg[first + d : first + d + 1, :] = jnp.sum(accs[d], axis=0, keepdims=True)
    apk[2, 0:1, 0:count] = to_row(jnp.sum(seg[...], axis=1, keepdims=True))
    to_plates(apk.at[2], gslots.at[b], a_send.at[2], a_recv.at[2])
    gslots[b] = apk[2]
    wait_bytes(gslots.at[pl.ds(0, np_ - 1)], a_recv.at[2])
    wait_bytes(gslots.at[pl.ds(0, np_ - 1)], a_send.at[2])
    sums = gslots[0, 0:1, 0:count]
    for j in range(1, np_):
        sums = sums + gslots[j, 0:1, 0:count]
    out_grads[...] = sums * (-CD * 64.0 / math.sqrt(rows * cols * np_ / count))


def on_device(load, disp, mass, wall_class, class_stiff, damper_map, damper_coef, band_tile, panel_store, owner, node_index):
    rows, cols = load.shape
    ns = lax.axis_size("storey")
    np_ = lax.axis_size("plate")
    nodes = node_index.shape[1]
    order = nodes * np_
    count = damper_coef.shape[0]
    width = max(cols, order, rows)
    wide = max(cols, np_ * rows)
    field = pltpu.VMEM((rows, cols), F32)
    square = pltpu.VMEM((cols, cols), BF16)
    grown = pltpu.VMEM((2, rows, np_ * rows), F32)
    dma = pltpu.SemaphoreType.DMA
    vmem = pl.BlockSpec(memory_space=pltpu.VMEM)
    smem = pl.BlockSpec(memory_space=pltpu.SMEM)
    new_disp, adj, shear, grads = pl.pallas_call(
        functools.partial(kernel, ns, np_),
        out_shape=(
            jax.ShapeDtypeStruct((rows, cols), F32),
            jax.ShapeDtypeStruct((rows, cols), F32),
            jax.ShapeDtypeStruct((1, rows), F32),
            jax.ShapeDtypeStruct((1, count), F32),
        ),
        in_specs=[vmem, vmem, vmem, vmem, smem, vmem, smem, vmem, vmem, smem, vmem],
        out_specs=(vmem, vmem, vmem, vmem),
        scratch_shapes=[field] * 9
        + [square] * 4
        + [grown] * 3
        + [
            pltpu.VMEM((8, wide), F32),
            pltpu.VMEM((2, 8, wide), F32),
            pltpu.VMEM((8, width), F32),
            pltpu.VMEM((np_, 8, width), F32),
            pltpu.VMEM((2, 8, width), F32),
            pltpu.VMEM((np_, order, order), F32),
            pltpu.VMEM((2, 2, 8, LANES), F32),
            pltpu.VMEM((2, np_, 8, LANES), F32),
            pltpu.VMEM((2, 2, np_ + 1, 8, LANES), F32),
            pltpu.VMEM((3, 8, LANES), F32),
            pltpu.VMEM((np_, 8, LANES), F32),
            pltpu.VMEM((ns, 8, LANES), F32),
            pltpu.VMEM((np_, 8, LANES), F32),
            pltpu.VMEM((count, LANES), F32),
            dma, dma, dma((2,)), dma((2,)), dma, dma, dma((2,)), dma((2,)),
            dma((2,)), dma((2,)), dma((2, 2)), dma((2, 2)), dma((3,)), dma((3,)),
        ],
        compiler_params=pltpu.CompilerParams(
            collective_id=0, has_side_effects=True, vmem_limit_bytes=48 * 1024 * 1024
        ),
    )(load, disp, mass, wall_class, class_stiff, damper_map, damper_coef, band_tile, panel_store, owner, node_index)
    return new_disp, adj, shear.reshape(rows), grads.reshape(count)


def solution(mesh):
    grid = P("storey", "plate")
    return jax.shard_map(
        on_device,
        mesh=mesh,
        in_specs=(grid, grid, grid, grid, P(), grid, P("storey"), grid, grid, P("storey"), grid),
        out_specs=(grid, grid, P("storey"), P("storey")),
        check_vma=False,
    )
```

time: 426 us -> 89.5 us (0.21)
  blocking collectives: 144 us -> 0 us
  starting transfers between devices: 102 us -> 0 us
  Pallas kernels: 0 us -> 78.5 us
  other arithmetic: 61 us -> 0 us
  waiting for transfers between devices: 50.3 us -> 0 us
  local copies, waits for them, and re-layouts: 34 us -> 9.25 us
  between operations: 16.9 us -> 1.38 us
  matrix products: 14.1 us -> 0 us
    unnamed x14 -> x0, blocking collectives: 130 us -> none
    ppermute x44 -> x0, starting transfers between devices: 101 us -> none  [the longest x22 73 us: with_halo(): before = lax.ppermute(last, axis, up)]
    pallas_call x0 -> x1, Pallas kernels: none -> 78.5 us  [on_device(): pl.pallas_call(functools.partial(kernel, ns, np_), out_shape=(jax.ShapeDt...]
    ppermute x44 -> x0, waiting for transfers between devices: 49.7 us -> none  [the longest x22 41.7 us: with_halo(): after = lax.ppermute(first, axis, down)]
    sub x11 -> x0, other arithmetic: 17.5 us -> none  [the longest x6 16.2 us: on_device(): resid = load - (diag * new_disp - stiff * neighbours(new_disp))]
    reduce_sum x22 -> x0, other arithmetic: 15.2 us -> none  [the longest x8 7.38 us: one_block(): return jnp.sum(jnp.where(match, coef[:, None, None], 0.0), axis=0)]
    mul x9 -> x0, other arithmetic: 14.8 us -> none  [the longest x5 12.8 us: on_device(): resid = target - (diag * adjoint - neighbours(stiff * adjoint))]
    psum x2 -> x0, blocking collectives: 14.5 us -> none  [the longest x1 7.24 us: on_device(): lax.psum(partial_force, 'plate')]
  transfers between devices with their start and end apart: 45 -> 0, of which waited for: 21 -> 0; matrix products, arithmetic and copies ran while one was open for 5% -> 0% of each run, Pallas kernels for 0% -> 0%
where the time goes in v1:
time: 89.5 us; the launch traced here: 89.1 us
  Pallas kernels  78.5 us (88%)
  local copies, waits for them, and re-layouts  9.25 us (10%)
  between operations  1.38 us (2%)
    pallas_call x1, Pallas kernels, on_device(): pl.pallas_call(functools.partial(kernel, ns, np_), out_shape=(jax.ShapeDt...  78.5 us
    unnamed x24, local copies, waits for them, and re-layouts  9.25 us

profile of v1, /device:TPU:0, one launch (start us, length us, event | category | flops | bytes accessed | tf_op | source)
XLA Modules:
  0.0 89.1 jit_solution(18084805020128269184)
XLA Ops:
  0.6 0.0 copy-start.9
  0.6 0.0 copy-start.8
  0.7 0.0 copy-start.7
  1.3 0.0 copy-done.9
  1.3 0.0 copy-done.8
  1.4 0.0 copy-done.7
  1.4 0.0 copy-start
  1.4 1.2 %copy-done = f32[512,512]{1,0:T(8,128)S(1)} copy-done((f32[512,512]{1,0:T(8,128)S(1)}, f32[512,512]{1,0:T(8,128)}, u32[]{:S(2)}) %copy-start) | copy-done | bytes 1048600
  2.6 0.0 copy-start.1
  2.6 0.9 %copy-done.1 = f32[128,512]{1,0:T(8,128)S(1)} copy-done((f32[128,512]{1,0:T(8,128)S(1)}, f32[128,512]{1,0:T(8,128)}, u32[]{:S(2)}) %copy-start.1) | copy-done | bytes 262168
  3.5 0.0 copy-start.2
  3.5 0.9 %copy-done.2 = f32[128,512]{1,0:T(8,128)S(1)} copy-done((f32[128,512]{1,0:T(8,128)S(1)}, f32[128,512]{1,0:T(8,128)}, u32[]{:S(2)}) %copy-start.2) | copy-done | bytes 262168
  4.5 0.0 copy-start.3
  4.5 0.9 %copy-done.3 = f32[128,512]{1,0:T(8,128)S(1)} copy-done((f32[128,512]{1,0:T(8,128)S(1)}, f32[128,512]{1,0:T(8,128)}, u32[]{:S(2)}) %copy-start.3) | copy-done | bytes 262168
  5.4 0.0 copy-start.4
  5.4 0.9 %copy-done.4 = s32[128,512]{1,0:T(8,128)S(1)} copy-done((s32[128,512]{1,0:T(8,128)S(1)}, s32[128,512]{1,0:T(8,128)}, u32[]{:S(2)}) %copy-start.4) | copy-done | bytes 262168
  6.4 0.0 copy-start.5
  6.4 0.9 %copy-done.5 = s32[128,512]{1,0:T(8,128)S(1)} copy-done((s32[128,512]{1,0:T(8,128)S(1)}, s32[128,512]{1,0:T(8,128)}, u32[]{:S(2)}) %copy-start.5) | copy-done | bytes 262168
  7.3 0.0 copy-start.6
  7.3 0.8 copy-done.6
  8.2 78.5 %shard_map.138 = (f32[128,512]{1,0:T(8,128)S(1)}, f32[128,512]{1,0:T(8,128)S(1)}, f32[1,128]{1,0:T(1,128)S(1)}, f32[1,64]{1,0:T(1,128)S(1)}) custom-call(f32[128,512]{1,0:T(8,128)S(1)} %copy-done.1, f32[128,512]{1,0:T(8,128)S(1)} %copy-done.2, f32[128,512]{1,0:T(8,128)S(1)} %copy-done.3, s32[128,512]{1,0:T(8,128)S(1)} %copy-done.4, f32[4]{0:T(128)S(1)} %copy-done.7, ...), custom_call_target="tpu_custom_call" | custom-call | tf_op jit(solution)/shard_map/pallas_call | solution.py:401
  86.7 0.7 copy.20
  87.4 0.7 copy.21
  88.1 0.5 copy.22
  88.6 0.5 copy.23
Async XLA Ops:
  0.6 0.7 copy-start.9
  0.6 0.7 copy-start.8
  0.7 0.7 copy-start.7
  1.4 1.2 %copy-start = (f32[512,512]{1,0:T(8,128)S(1)}, f32[512,512]{1,0:T(8,128)}, u32[]{:S(2)}) copy-start(f32[512,512]{1,0:T(8,128)} %tile.1) | copy-start | bytes 3145732
  2.6 0.9 %copy-start.1 = (f32[128,512]{1,0:T(8,128)S(1)}, f32[128,512]{1,0:T(8,128)}, u32[]{:S(2)}) copy-start(f32[128,512]{1,0:T(8,128)} %load.1) | copy-start | bytes 786436
  3.5 0.9 %copy-start.2 = (f32[128,512]{1,0:T(8,128)S(1)}, f32[128,512]{1,0:T(8,128)}, u32[]{:S(2)}) copy-start(f32[128,512]{1,0:T(8,128)} %disp.1) | copy-start | bytes 786436
  4.5 0.9 %copy-start.3 = (f32[128,512]{1,0:T(8,128)S(1)}, f32[128,512]{1,0:T(8,128)}, u32[]{:S(2)}) copy-start(f32[128,512]{1,0:T(8,128)} %mass.1) | copy-start | bytes 786436
  5.4 0.9 %copy-start.4 = (s32[128,512]{1,0:T(8,128)S(1)}, s32[128,512]{1,0:T(8,128)}, u32[]{:S(2)}) copy-start(s32[128,512]{1,0:T(8,128)} %wall.1) | copy-start | bytes 786436
  6.4 0.9 %copy-start.5 = (s32[128,512]{1,0:T(8,128)S(1)}, s32[128,512]{1,0:T(8,128)}, u32[]{:S(2)}) copy-start(s32[128,512]{1,0:T(8,128)} %dmap.1) | copy-start | bytes 786436
  7.3 0.8 copy-start.6

commit v2 on v1

--- a/solution.py
+++ b/solution.py
@@ -17,6 +17,7 @@
 F32 = jnp.float32
 BF16 = jnp.bfloat16
 LANES = 128
+FULL = 63 * 1024 * 1024
 
 
 def iota(shape, dim):
@@ -44,16 +45,18 @@
 
 def kernel(
     ns, np_,
-    load, disp, mass, wall, cstiff, dmap, coef, tile, panel, owner, nidx,
+    load_in, disp_in, mass_in, wall_in, cstiff, dmap_in, coef, tile_in, panel, owner, nidx,
     out_disp, out_adj, out_shear, out_grads,
+    load, disp, mass, wall, dmap, tile, in_sem, out_sem, found,
     stiff, diag, rdiag, cm, place, x, r, q, z,
+    k_own, k_up, k_down,
     t_hi, t_lo, tt_hi, tt_lo,
     pan_own, pan_left, pan_right, info_out, info_in,
     spk, sslots, snb, pslots,
-    pk, slots, nbs,
+    gpk, cpk, rpk, slots, nbs, cols_in, rows_in,
     apk, fslots, tslots, gslots, seg,
     s_send, s_recv, n_send, n_recv, p_send, p_recv, i_send, i_recv,
-    r_send, r_recv, rn_send, rn_recv, a_send, a_recv,
+    r_send, r_recv, rn_send, rn_recv, c_send, c_recv, e_send, e_recv, a_send, a_recv,
 ):
     rows, cols = load.shape
     nodes = nidx.shape[1]
@@ -66,6 +69,12 @@
     has = (s > 0, s < ns - 1)
     beside = (s - 1, s + 1)
 
+    ways = ((wall_in, wall), (disp_in, disp), (mass_in, mass), (dmap_in, dmap), (tile_in, tile), (load_in, load))
+    loads = [pltpu.make_async_copy(src, dst, in_sem.at[i]) for i, (src, dst) in enumerate(ways)]
+    loads.append(pltpu.make_async_copy(panel, pslots.at[b], in_sem.at[len(ways)]))
+    for copy in loads:
+        copy.start()
+
     barrier = pltpu.get_barrier_semaphore()
     for d in range(1, np_):
         pl.semaphore_signal(barrier, inc=1, device_id=(s, (b + d) % np_), device_id_type=MESH)
@@ -89,6 +98,9 @@
             push(src, dst, send, recv, (s, (b + d) % np_))
 
     to_plates(panel, pslots.at[b], p_send, p_recv)
+
+    loads[0].wait()
+    loads[1].wait()
 
     level = jnp.zeros((rows, cols), F32)
     for c in range(cstiff.shape[0]):
@@ -113,9 +125,20 @@
         def _():
             snb[way] = jnp.zeros(snb.shape[1:], F32)
             info_in[way] = jnp.zeros(info_in.shape[1:], F32)
-            nbs[0, way] = jnp.zeros(nbs.shape[2:], F32)
-            nbs[1, way] = jnp.zeros(nbs.shape[2:], F32)
-
+            for i in range(2):
+                nbs[i, way] = jnp.zeros(nbs.shape[2:], F32)
+                rows_in[i, way] = jnp.zeros(rows_in.shape[2:], F32)
+
+    flank = (b > 0, b < np_ - 1)
+    flanking = (b - 1, b + 1)
+    for side in range(2):
+        @pl.when(jnp.logical_not(flank[side]))
+        def _():
+            for i in range(2):
+                cols_in[i, side] = jnp.zeros(cols_in.shape[2:], F32)
+
+    loads[2].wait()
+    loads[3].wait()
     cm[...] = CM * mass[...]
 
     def lookup(i, carry):
@@ -130,10 +153,12 @@
         return carry
 
     lax.fori_loop(0, rows // 8, lookup, 0)
+    loads[4].wait()
     t_hi[...], t_lo[...] = split(tile[...])
     tt_hi[...], tt_lo[...] = split(tile[...].T)
 
-    pslots[b] = panel[...]
+    loads[5].wait()
+    loads[6].wait()
     sslots[b] = spk[...]
     wait_bytes(sslots.at[pl.ds(0, np_ - 1)], s_recv)
     wait_bytes(pslots.at[pl.ds(0, np_ - 1)], p_recv)
@@ -196,6 +221,11 @@
     lane = iota((rows, cols), 1)
     line = iota((rows, cols), 0)
 
+    def sideways(v):
+        return jnp.where(lane == 0, 0.0, pltpu.roll(v, 1, 1)) + jnp.where(
+            lane == cols - 1, 0.0, pltpu.roll(v, cols - 1, 1)
+        )
+
     def neighbours(v, top, bottom, left, right):
         above = jnp.where(line == 0, top, pltpu.roll(v, 1, 0))
         below = jnp.where(line == rows - 1, bottom, pltpu.roll(v, rows - 1, 0))
@@ -203,38 +233,58 @@
         east = jnp.where(lane == cols - 1, right, pltpu.roll(v, cols - 1, 1))
         return above + below + west + east
 
-    def send_round(mode, par):
+    spot = place[...]
+    k_own[0] = stiff[...] * sideways(spot) - diag[...] * spot
+    k_up[0] = jnp.where(line == 0, 0.0, stiff[...] * pltpu.roll(spot, 1, 0))
+    k_down[0] = jnp.where(line == rows - 1, 0.0, stiff[...] * pltpu.roll(spot, rows - 1, 0))
+    held = stiff[...] * spot
+    k_own[1] = sideways(held) - diag[...] * spot
+    k_up[1] = jnp.where(line == 0, 0.0, pltpu.roll(held, 1, 0))
+    k_down[1] = jnp.where(line == rows - 1, 0.0, pltpu.roll(held, rows - 1, 0))
+
+    def send_round(mode, par, edges):
         resid = r[...]
+        gpk[par, 0:1, :] = to_row(jnp.sum(resid * place[...], axis=1, keepdims=True))
+        for way in range(2):
+            @pl.when(has[way])
+            def _():
+                for d in range(np_):
+                    push(
+                        gpk.at[par], nbs.at[par, 1 - way, b], rn_send.at[par, way],
+                        rn_recv.at[par, 1 - way], (beside[way], (b + d) % np_),
+                    )
+        to_plates(gpk.at[par], slots.at[par, b], r_send.at[par], r_recv.at[par])
+        slots[par, b] = gpk[par]
         hi, lo = split(resid * rdiag[...])
         wh, wl = (tt_hi, tt_lo) if mode else (t_hi, t_lo)
         both = jnp.dot(jnp.concatenate([hi, lo], axis=0), wh[...], preferred_element_type=F32)
         band = both[:rows] + both[rows:] + jnp.dot(hi, wl[...], preferred_element_type=F32)
         z[...] = x[...] + band
-        here = pk.at[par]
+        if not edges:
+            return
         edge = (lambda *at: z[at] * stiff[at]) if mode else (lambda *at: z[at])
         first, last = edge(slice(0, 1), slice(None)), edge(slice(rows - 1, rows), slice(None))
         for t in range(pieces):
-            here[1, t : t + 1, :] = first[:, t * LANES : (t + 1) * LANES]
-            here[1, pieces + t : pieces + t + 1, :] = last[:, t * LANES : (t + 1) * LANES]
-        here[0, 0:1, :] = to_row(jnp.sum(resid * place[...], axis=1, keepdims=True))
-        here[0, 1:2, :] = to_row(edge(slice(None), slice(0, 1)))
-        here[0, 2:3, :] = to_row(edge(slice(None), slice(cols - 1, cols)))
-        to_plates(here.at[0], slots.at[par, b], r_send.at[par], r_recv.at[par])
+            rpk[par, t : t + 1, :] = first[:, t * LANES : (t + 1) * LANES]
+            rpk[par, pieces + t : pieces + t + 1, :] = last[:, t * LANES : (t + 1) * LANES]
         for way in range(2):
             @pl.when(has[way])
             def _():
-                for d in range(np_):
-                    push(
-                        here.at[0], nbs.at[par, 1 - way, b], rn_send.at[par, way],
-                        rn_recv.at[par, 1 - way], (beside[way], (b + d) % np_),
-                    )
                 push(
-                    here.at[1], nbs.at[par, 1 - way, np_], rn_send.at[par, way],
-                    rn_recv.at[par, 1 - way], (beside[way], b),
+                    rpk.at[par], rows_in.at[par, 1 - way], e_send.at[par, way],
+                    e_recv.at[par, 1 - way], (beside[way], b),
                 )
-        slots[par, b] = here[0]
-
-    def wait_round(par):
+        cpk[par, 0:1, :] = to_row(edge(slice(None), slice(0, 1)))
+        cpk[par, 1:2, :] = to_row(edge(slice(None), slice(cols - 1, cols)))
+        for side in range(2):
+            @pl.when(flank[side])
+            def _():
+                push(
+                    cpk.at[par], cols_in.at[par, 1 - side], c_send.at[par, side],
+                    c_recv.at[par, 1 - side], (s, flanking[side]),
+                )
+
+    def wait_round(par, edges):
         wait_bytes(slots.at[par, pl.ds(0, np_ - 1)], r_recv.at[par])
         wait_bytes(slots.at[par, pl.ds(0, np_ - 1)], r_send.at[par])
         for way in range(2):
@@ -242,6 +292,15 @@
             def _():
                 wait_bytes(nbs.at[par, way], rn_recv.at[par, way])
                 wait_bytes(nbs.at[par, way], rn_send.at[par, way])
+                if edges:
+                    wait_bytes(rpk.at[par], e_recv.at[par, way])
+                    wait_bytes(rpk.at[par], e_send.at[par, way])
+        if edges:
+            for side in range(2):
+                @pl.when(flank[side])
+                def _():
+                    wait_bytes(cpk.at[par], c_recv.at[par, side])
+                    wait_bytes(cpk.at[par], c_send.at[par, side])
 
     def applied(mat, mode, par, extra=None):
         total = extra
@@ -251,7 +310,11 @@
         return jnp.sum(total, axis=1, keepdims=True)
 
     def finish(mode, par):
-        x[...] = z[...] + applied(pan_own, mode, par) * place[...]
+        coarse = jnp.broadcast_to(applied(pan_own, mode, par), (rows, LANES))
+        for t in range(pieces):
+            part = slice(t * LANES, (t + 1) * LANES)
+            x[:, part] = z[:, part] + coarse * place[:, part]
+        return coarse
 
     def side_row(mode, par, way):
         pan_row = 2 * mode + (1 - way)
@@ -260,18 +323,36 @@
             total = total + info_in[way, pan_row : pan_row + 1, j * rows : (j + 1) * rows] * nbs[par, way, j, 0:1, :]
         value = jnp.sum(total, axis=1, keepdims=True)
         base = pieces * (1 - way)
-        got = jnp.concatenate([nbs[par, way, np_, base + t : base + t + 1, :] for t in range(pieces)], axis=1)
+        got = jnp.concatenate([rows_in[par, way, base + t : base + t + 1, :] for t in range(pieces)], axis=1)
         return got + value * info_in[way, 4 + (1 - way) : 5 + (1 - way), 0:cols]
 
-    def halos(mode, par):
-        west = jnp.where(b > 0, eye * slots[par, left_slot, 2:3, :], 0.0)
-        east = jnp.where(b < np_ - 1, eye * slots[par, right_slot, 1:2, :], 0.0)
-        return (
-            side_row(mode, par, 0),
-            side_row(mode, par, 1),
-            applied(pan_left, mode, par, west),
-            applied(pan_right, mode, par, east),
-        )
+    def inner_resid(mode, base):
+        v = z[...]
+        zero = jnp.zeros((), F32)
+        if mode:
+            r[...] = base[...] - diag[...] * v + neighbours(stiff[...] * v, zero, zero, zero, zero)
+        else:
+            r[...] = base[...] - diag[...] * v + stiff[...] * neighbours(v, zero, zero, zero, zero)
+
+    def outer_resid(mode, par, coarse):
+        up, down = pltpu.roll(coarse, 1, 0), pltpu.roll(coarse, rows - 1, 0)
+        west = applied(pan_left, mode, par, eye * cols_in[par, 0, 1:2, :])
+        east = applied(pan_right, mode, par, eye * cols_in[par, 1, 0:1, :])
+        thin = iota((rows, LANES), 1)
+        for t in range(pieces):
+            part = slice(t * LANES, (t + 1) * LANES)
+            total = r[:, part] + coarse * k_own[mode, :, part]
+            total = total + up * k_up[mode, :, part] + down * k_down[mode, :, part]
+            if t == 0:
+                total = total + jnp.where(thin == 0, west if mode else west * stiff[:, part], 0.0)
+            if t == pieces - 1:
+                total = total + jnp.where(thin == LANES - 1, east if mode else east * stiff[:, part], 0.0)
+            r[:, part] = total
+        top, bottom = side_row(mode, par, 0), side_row(mode, par, 1)
+        if mode == 0:
+            top, bottom = top * stiff[0:1, :], bottom * stiff[rows - 1 : rows, :]
+        r[0:1, :] = r[0:1, :] + top
+        r[rows - 1 : rows, :] = r[rows - 1 : rows, :] + bottom
 
     x[...] = disp[...]
     west = jnp.where(b > 0, to_col(sslots[left_slot][4:5, 0:rows]), 0.0)
@@ -281,7 +362,8 @@
 
     def primal(k, carry):
         par = lax.rem(k, 2)
-        send_round(0, par)
+        send_round(0, par, True)
+        inner_resid(0, load)
 
         @pl.when(k == 0)
         def _():
@@ -291,18 +373,18 @@
                     wait_bytes(info_in.at[way], i_recv.at[way])
                     wait_bytes(info_out, i_send.at[way])
 
-        wait_round(par)
-        finish(0, par)
-        v = x[...]
-        r[...] = load[...] - (diag[...] * v - stiff[...] * neighbours(v, *halos(0, par)))
+        wait_round(par, True)
+        outer_resid(0, par, finish(0, par))
         return carry
 
     lax.fori_loop(0, ITERS - 1, primal, 0)
     par = (ITERS - 1) % 2
-    send_round(0, par)
-    wait_round(par)
+    send_round(0, par, False)
+    wait_round(par, False)
     finish(0, par)
-    out_disp[...] = x[...]
+    found[...] = x[...]
+    give_disp = pltpu.make_async_copy(found, out_disp, out_sem.at[0])
+    give_disp.start()
 
     apk[...] = jnp.zeros(apk.shape, F32)
     apk[0, 0:1, :] = to_row(jnp.sum(cm[...] * x[...], axis=1, keepdims=True))
@@ -341,20 +423,20 @@
 
     def adjoint(k, carry):
         par = lax.rem(k, 2)
-        send_round(1, par)
-        wait_round(par)
-        finish(1, par)
-        v = x[...]
-        r[...] = q[...] - (diag[...] * v - neighbours(stiff[...] * v, *halos(1, par)))
+        send_round(1, par, True)
+        inner_resid(1, q)
+        wait_round(par, True)
+        outer_resid(1, par, finish(1, par))
         return carry
 
     lax.fori_loop(0, ITERS - 1, adjoint, 0)
-    send_round(1, par)
-    wait_round(par)
+    send_round(1, par, False)
+    wait_round(par, False)
     finish(1, par)
-    out_adj[...] = x[...]
-
-    z[...] = x[...] * out_disp[...]
+    give_adj = pltpu.make_async_copy(x, out_adj, out_sem.at[1])
+    give_adj.start()
+
+    z[...] = x[...] * found[...]
     group = 8
     for first in range(0, count, group):
         def gather(i, accs):
@@ -381,6 +463,16 @@
     for j in range(1, np_):
         sums = sums + gslots[j, 0:1, 0:count]
     out_grads[...] = sums * (-CD * 64.0 / math.sqrt(rows * cols * np_ / count))
+    give_disp.wait()
+    give_adj.wait()
+
+
+def deliver(*refs):
+    copies = [pltpu.make_async_copy(refs[i], refs[4 + i], refs[8].at[i]) for i in range(4)]
+    for copy in copies:
+        copy.start()
+    for copy in copies:
+        copy.wait()
 
 
 def on_device(load, disp, mass, wall_class, class_stiff, damper_map, damper_coef, band_tile, panel_store, owner, node_index):
@@ -398,6 +490,9 @@
     dma = pltpu.SemaphoreType.DMA
     vmem = pl.BlockSpec(memory_space=pltpu.VMEM)
     smem = pl.BlockSpec(memory_space=pltpu.SMEM)
+    hbm = pl.BlockSpec(memory_space=pltpu.HBM)
+    ids = pltpu.VMEM((rows, cols), jnp.int32)
+    shapes = ((rows, cols), (rows, cols), (rows,), (count,))
     new_disp, adj, shear, grads = pl.pallas_call(
         functools.partial(kernel, ns, np_),
         out_shape=(
@@ -406,9 +501,13 @@
             jax.ShapeDtypeStruct((1, rows), F32),
             jax.ShapeDtypeStruct((1, count), F32),
         ),
-        in_specs=[vmem, vmem, vmem, vmem, smem, vmem, smem, vmem, vmem, smem, vmem],
-        out_specs=(vmem, vmem, vmem, vmem),
-        scratch_shapes=[field] * 9
+        in_specs=[hbm, hbm, hbm, hbm, smem, hbm, smem, hbm, hbm, smem, vmem],
+        out_specs=(hbm, hbm, vmem, vmem),
+        scratch_shapes=[field] * 3
+        + [ids] * 2
+        + [pltpu.VMEM((cols, cols), F32), dma((7,)), dma((2,)), field]
+        + [field] * 9
+        + [pltpu.VMEM((2, rows, cols), F32)] * 3
         + [square] * 4
         + [grown] * 3
         + [
@@ -418,22 +517,33 @@
             pltpu.VMEM((np_, 8, width), F32),
             pltpu.VMEM((2, 8, width), F32),
             pltpu.VMEM((np_, order, order), F32),
+            pltpu.VMEM((2, 8, LANES), F32),
+            pltpu.VMEM((2, 8, LANES), F32),
+            pltpu.VMEM((2, 8, LANES), F32),
+            pltpu.VMEM((2, np_, 8, LANES), F32),
+            pltpu.VMEM((2, 2, np_, 8, LANES), F32),
             pltpu.VMEM((2, 2, 8, LANES), F32),
-            pltpu.VMEM((2, np_, 8, LANES), F32),
-            pltpu.VMEM((2, 2, np_ + 1, 8, LANES), F32),
+            pltpu.VMEM((2, 2, 8, LANES), F32),
             pltpu.VMEM((3, 8, LANES), F32),
             pltpu.VMEM((np_, 8, LANES), F32),
             pltpu.VMEM((ns, 8, LANES), F32),
             pltpu.VMEM((np_, 8, LANES), F32),
             pltpu.VMEM((count, LANES), F32),
             dma, dma, dma((2,)), dma((2,)), dma, dma, dma((2,)), dma((2,)),
-            dma((2,)), dma((2,)), dma((2, 2)), dma((2, 2)), dma((3,)), dma((3,)),
+            dma((2,)), dma((2,)), *[dma((2, 2))] * 6, dma((3,)), dma((3,)),
         ],
         compiler_params=pltpu.CompilerParams(
-            collective_id=0, has_side_effects=True, vmem_limit_bytes=48 * 1024 * 1024
+            collective_id=0, has_side_effects=True, vmem_limit_bytes=FULL
         ),
     )(load, disp, mass, wall_class, class_stiff, damper_map, damper_coef, band_tile, panel_store, owner, node_index)
-    return new_disp, adj, shear.reshape(rows), grads.reshape(count)
+    return pl.pallas_call(
+        deliver,
+        out_shape=tuple(jax.ShapeDtypeStruct(shape, F32) for shape in shapes),
+        in_specs=[hbm] * 4,
+        out_specs=(hbm,) * 4,
+        scratch_shapes=[dma((4,))],
+        compiler_params=pltpu.CompilerParams(vmem_limit_bytes=FULL),
+    )(new_disp, adj, shear.reshape(rows), grads.reshape(count))
 
 
 def solution(mesh):

time: 89.5 us -> 92.2 us (1.030)
  Pallas kernels: 78.5 us -> 90.7 us
  local copies, waits for them, and re-layouts: 9.25 us -> 0 us
    pallas_call x0 -> x1, Pallas kernels: none -> 17.1 us  [on_device(): pl.pallas_call(deliver, out_shape=tuple((jax.ShapeDtypeStruct(shape, F32)...]
    unnamed x24 -> x0, local copies, waits for them, and re-layouts: 9.25 us -> none
    pallas_call x1, Pallas kernels: 78.5 us -> 73.7 us  [on_device(): pl.pallas_call(functools.partial(kernel, ns, np_), out_shape=(jax.ShapeDt...]
where the time goes in v2:
time: 92.2 us; the launch traced here: 92 us
  Pallas kernels  90.7 us (98%)
  between operations  1.29 us (1%)
    pallas_call x1, Pallas kernels, on_device(): pl.pallas_call(functools.partial(kernel, ns, np_), out_shape=(jax.ShapeDt...  73.7 us
    pallas_call x1, Pallas kernels, on_device(): pl.pallas_call(deliver, out_shape=tuple((jax.ShapeDtypeStruct(shape, F32)...  17.1 us

profile of v2, /device:TPU:0, one launch (start us, length us, event | category | flops | bytes accessed | tf_op | source)
XLA Modules:
  0.0 92.0 jit_solution(10241841551935945925)
XLA Ops:
  1.3 73.7 %shard_map.138 = (f32[128,512]{1,0:T(8,128)}, f32[128,512]{1,0:T(8,128)}, f32[1,128]{1,0:T(1,128)}, f32[1,64]{1,0:T(1,128)}) custom-call(f32[128,512]{1,0:T(8,128)} %load_in.1, f32[128,512]{1,0:T(8,128)} %disp_in.1, f32[128,512]{1,0:T(8,128)} %mass_in.1, s32[128,512]{1,0:T(8,128)} %wall_in.1, f32[4]{0:T(128)} %cstiff.1, s32[128,512]{1,0:T(8,128)} %dmap_in.1, ...), custom_call_target="tpu_custom_call" | custom-call | tf_op jit(solution)/shard_map/pallas_call | solution.py:496
  75.0 17.1 %shard_map.139 = (f32[128,512]{1,0:T(8,128)}, f32[128,512]{1,0:T(8,128)}, f32[128]{0:T(128)}, f32[64]{0:T(128)}) custom-call(f32[128,512]{1,0:T(8,128)} %get-tuple-element.8.refs_0_, f32[128,512]{1,0:T(8,128)} %get-tuple-element.9.refs_1_, f32[128]{0:T(128)} %bitcast.2, f32[64]{0:T(128)} %bitcast.3), custom_call_target="tpu_custom_call" | custom-call | tf_op jit(solution)/shard_map/pallas_call | solution.py:539

commit v3 on v2

--- a/solution.py
+++ b/solution.py
@@ -51,8 +51,8 @@
     stiff, diag, rdiag, cm, place, x, r, q, z,
     k_own, k_up, k_down,
     t_hi, t_lo, tt_hi, tt_lo,
-    pan_own, pan_left, pan_right, info_out, info_in,
-    spk, sslots, snb, pslots,
+    pan_own, pan_left, pan_right, pan_force, grown, used, info_out, info_in,
+    spk, sslots, snb, pslots, epk, extras, x_send, x_recv,
     gpk, cpk, rpk, slots, nbs, cols_in, rows_in,
     apk, fslots, tslots, gslots, seg,
     s_send, s_recv, n_send, n_recv, p_send, p_recv, i_send, i_recv,
@@ -69,7 +69,7 @@
     has = (s > 0, s < ns - 1)
     beside = (s - 1, s + 1)
 
-    ways = ((wall_in, wall), (disp_in, disp), (mass_in, mass), (dmap_in, dmap), (tile_in, tile), (load_in, load))
+    ways = ((disp_in, disp), (wall_in, wall), (mass_in, mass), (dmap_in, dmap), (tile_in, tile), (load_in, load))
     loads = [pltpu.make_async_copy(src, dst, in_sem.at[i]) for i, (src, dst) in enumerate(ways)]
     loads.append(pltpu.make_async_copy(panel, pslots.at[b], in_sem.at[len(ways)]))
     for copy in loads:
@@ -99,47 +99,43 @@
 
     to_plates(panel, pslots.at[b], p_send, p_recv)
 
+    at_own = nidx[...].astype(F32)
+    tiled = (iota((nodes, order), 1) % nodes == iota((nodes, order), 0)).astype(F32)
+    spk[2:3, 0:order] = jnp.dot(at_own, tiled, precision=HIGH, preferred_element_type=F32)
     loads[0].wait()
+    spk[0:1, 0:cols] = disp[0:1, :]
+    spk[1:2, 0:cols] = disp[rows - 1 : rows, :]
+    spk[3:4, 0:rows] = to_row(disp[:, 0:1])
+    spk[4:5, 0:rows] = to_row(disp[:, cols - 1 : cols])
+    to_plates(spk, sslots.at[b], s_send, s_recv)
+    flank = (b > 0, b < np_ - 1)
+    flanking = (b - 1, b + 1)
+    for way in range(2):
+        @pl.when(has[way])
+        def _():
+            push(spk, snb.at[1 - way], n_send.at[way], n_recv.at[1 - way], (beside[way], b))
+
+        @pl.when(jnp.logical_not(has[way]))
+        def _():
+            snb[way] = jnp.zeros(snb.shape[1:], F32)
+            for i in range(2):
+                info_in[i, way] = jnp.zeros(info_in.shape[2:], F32)
+                nbs[i, way] = jnp.zeros(nbs.shape[2:], F32)
+                rows_in[i, way] = jnp.zeros(rows_in.shape[2:], F32)
+
+        @pl.when(jnp.logical_not(flank[way]))
+        def _():
+            for i in range(2):
+                cols_in[i, way] = jnp.zeros(cols_in.shape[2:], F32)
+
     loads[1].wait()
-
     level = jnp.zeros((rows, cols), F32)
     for c in range(cstiff.shape[0]):
         level = jnp.where(wall[...] == c, cstiff[c], level)
     stiff[...] = KF * level
-    spk[...] = jnp.zeros(spk.shape, F32)
-    spk[0:1, 0:cols] = disp[0:1, :]
-    spk[1:2, 0:cols] = disp[rows - 1 : rows, :]
-    tiled = (iota((nodes, order), 1) % nodes == iota((nodes, order), 0)).astype(F32)
-    spk[2:3, 0:order] = jnp.dot(nidx[...].astype(F32), tiled, precision=HIGH, preferred_element_type=F32)
-    spk[3:4, 0:rows] = to_row(disp[:, 0:1])
-    spk[4:5, 0:rows] = to_row(disp[:, cols - 1 : cols])
-    spk[5:6, 0:rows] = to_row(stiff[:, 0:1])
-    spk[6:7, 0:rows] = to_row(stiff[:, cols - 1 : cols])
-    to_plates(spk, sslots.at[b], s_send, s_recv)
-    for way in range(2):
-        @pl.when(has[way])
-        def _():
-            push(spk, snb.at[1 - way], n_send.at[way], n_recv.at[1 - way], (beside[way], b))
-
-        @pl.when(jnp.logical_not(has[way]))
-        def _():
-            snb[way] = jnp.zeros(snb.shape[1:], F32)
-            info_in[way] = jnp.zeros(info_in.shape[1:], F32)
-            for i in range(2):
-                nbs[i, way] = jnp.zeros(nbs.shape[2:], F32)
-                rows_in[i, way] = jnp.zeros(rows_in.shape[2:], F32)
-
-    flank = (b > 0, b < np_ - 1)
-    flanking = (b - 1, b + 1)
-    for side in range(2):
-        @pl.when(jnp.logical_not(flank[side]))
-        def _():
-            for i in range(2):
-                cols_in[i, side] = jnp.zeros(cols_in.shape[2:], F32)
-
     loads[2].wait()
+    cm[...] = CM * mass[...]
     loads[3].wait()
-    cm[...] = CM * mass[...]
 
     def lookup(i, carry):
         part = pl.ds(pl.multiple_of(i * 8, 8), 8)
@@ -155,7 +151,6 @@
     lax.fori_loop(0, rows // 8, lookup, 0)
     loads[4].wait()
     t_hi[...], t_lo[...] = split(tile[...])
-    tt_hi[...], tt_lo[...] = split(tile[...].T)
 
     loads[5].wait()
     loads[6].wait()
@@ -171,51 +166,82 @@
     wait_bytes(pslots.at[pl.ds(0, np_ - 1)], p_send)
 
     root = owner[0]
-    used = jnp.zeros((order, order), F32)
+    used_now = jnp.zeros((order, order), F32)
+    for j in range(np_):
+        used_now = jnp.where(root == j, pslots[j], used_now)
+    used[...] = used_now
     lane_node = iota((1, order), 1) // nodes
-    where_all = jnp.zeros((1, order), F32)
-    for j in range(np_):
-        used = jnp.where(root == j, pslots[j], used)
-        where_all = jnp.where(lane_node == j, sslots[j, 2:3, 0:order], where_all)
-    at = where_all.astype(jnp.int32)
     shift = cols.bit_length() - 1
-    at_row = jnp.right_shift(at, shift)
-    at_col = jnp.bitwise_and(at, cols - 1)
-    at_row_col = to_col(at_row.astype(F32)).astype(jnp.int32)
-    wide = (order, np_ * rows)
-    spread = (
-        (iota(wide, 1) % rows == at_row_col) & (iota(wide, 1) // rows == iota(wide, 0) // nodes)
-    ).astype(F32)
     tall = (rows, order)
-    at_h = iota(tall, 0) == at_row
-    pick_own = (at_h & (lane_node == b)).astype(F32)
-    pick_left = (at_h & (lane_node == b - 1) & (at_col == cols - 1)).astype(F32)
-    pick_right = (at_h & (lane_node == b + 1) & (at_col == 0)).astype(F32)
-    col_of = jnp.sum(pick_own * (at_col + 1).astype(F32), axis=1, keepdims=True).astype(jnp.int32) - 1
-    place[...] = (iota((rows, cols), 1) == col_of).astype(F32)
     left_slot = jnp.maximum(b - 1, 0)
     right_slot = jnp.minimum(b + 1, np_ - 1)
-    stiff_left = to_col(sslots[left_slot][6:7, 0:rows])
-    stiff_right = to_col(sslots[right_slot][5:6, 0:rows])
-    stiff_own = jnp.sum(place[...] * stiff[...], axis=1, keepdims=True)
-    info_out[...] = jnp.zeros(info_out.shape, F32)
-    info_out[4:5, 0:cols] = place[0:1, :]
-    info_out[5:6, 0:cols] = place[rows - 1 : rows, :]
-    for mode in range(2):
-        grown = jnp.dot(used.T if mode else used, spread, precision=HIGH, preferred_element_type=F32)
-        own = jnp.dot(pick_own, grown, precision=HIGH, preferred_element_type=F32)
-        left = jnp.dot(pick_left, grown, precision=HIGH, preferred_element_type=F32)
-        right = jnp.dot(pick_right, grown, precision=HIGH, preferred_element_type=F32)
+
+    def places():
+        where_all = jnp.zeros((1, order), F32)
+        for j in range(np_):
+            where_all = jnp.where(lane_node == j, sslots[j, 2:3, 0:order], where_all)
+        at = where_all.astype(jnp.int32)
+        return jnp.right_shift(at, shift), jnp.bitwise_and(at, cols - 1)
+
+    def expand_columns(mode):
+        at_row, _ = places()
+        at_row_col = to_col(at_row.astype(F32)).astype(jnp.int32)
+        wide = (order, np_ * rows)
+        spread = (
+            (iota(wide, 1) % rows == at_row_col) & (iota(wide, 1) // rows == iota(wide, 0) // nodes)
+        ).astype(F32).astype(BF16)
+        hi, lo = split(used[...].T if mode else used[...])
+        both = jnp.dot(jnp.concatenate([hi, lo], axis=0), spread, preferred_element_type=F32)
+        grown[...] = both[:order] + both[order:]
+
+    def pick(mask):
+        hi, lo = split(grown[...])
+        ones = mask.astype(F32).astype(BF16)
+        return jnp.dot(ones, hi, preferred_element_type=F32) + jnp.dot(ones, lo, preferred_element_type=F32)
+
+    def expand_own(mode):
+        at_row, at_col = places()
+        mask = (iota(tall, 0) == at_row) & (lane_node == b)
+        if mode == 0:
+            col_of = jnp.sum(jnp.where(mask, (at_col + 1).astype(F32), 0.0), axis=1, keepdims=True)
+            place[...] = (iota((rows, cols), 1) == col_of.astype(jnp.int32) - 1).astype(F32)
+        own = pick(mask)
         pan_own[mode] = own
-        pan_left[mode] = left * stiff_left if mode else left
-        pan_right[mode] = right * stiff_right if mode else right
-        edge = own * stiff_own if mode else own
-        info_out[2 * mode : 2 * mode + 1, 0 : np_ * rows] = edge[0:1, :]
-        info_out[2 * mode + 1 : 2 * mode + 2, 0 : np_ * rows] = edge[rows - 1 : rows, :]
-    for way in range(2):
-        @pl.when(has[way])
-        def _():
-            push(info_out, info_in.at[1 - way], i_send.at[way], i_recv.at[1 - way], (beside[way], b))
+        if mode:
+            own = own * jnp.sum(place[...] * stiff[...], axis=1, keepdims=True)
+        info_out[mode, 0:1, 0 : np_ * rows] = own[0:1, :]
+        info_out[mode, 1:2, 0 : np_ * rows] = own[rows - 1 : rows, :]
+        info_out[mode, 2:3, 0:cols] = place[0:1, :]
+        info_out[mode, 3:4, 0:cols] = place[rows - 1 : rows, :]
+        for way in range(2):
+            @pl.when(has[way])
+            def _():
+                push(
+                    info_out.at[mode], info_in.at[mode, 1 - way], i_send.at[mode, way],
+                    i_recv.at[mode, 1 - way], (beside[way], b),
+                )
+
+    def wait_info(mode):
+        for way in range(2):
+            @pl.when(has[way])
+            def _():
+                wait_bytes(info_in.at[mode, way], i_recv.at[mode, way])
+                wait_bytes(info_out.at[mode], i_send.at[mode, way])
+
+    def expand_sides(mode):
+        at_row, at_col = places()
+        at_h = iota(tall, 0) == at_row
+        left = at_h & (lane_node == b - 1) & (at_col == cols - 1)
+        right = at_h & (lane_node == b + 1) & (at_col == 0)
+        if mode:
+            pan_left[mode] = pick(left) * to_col(extras[left_slot][1:2, 0:rows])
+            pan_right[mode] = pick(right) * to_col(extras[right_slot][0:1, 0:rows])
+        else:
+            pan_left[mode] = pick(left)
+            pan_right[mode] = pick(right)
+
+    expand_columns(0)
+    expand_own(0)
 
     eye = (iota((rows, rows), 0) == iota((rows, rows), 1)).astype(F32)
     lane = iota((rows, cols), 1)
@@ -233,14 +259,21 @@
         east = jnp.where(lane == cols - 1, right, pltpu.roll(v, cols - 1, 1))
         return above + below + west + east
 
-    spot = place[...]
-    k_own[0] = stiff[...] * sideways(spot) - diag[...] * spot
-    k_up[0] = jnp.where(line == 0, 0.0, stiff[...] * pltpu.roll(spot, 1, 0))
-    k_down[0] = jnp.where(line == rows - 1, 0.0, stiff[...] * pltpu.roll(spot, rows - 1, 0))
-    held = stiff[...] * spot
-    k_own[1] = sideways(held) - diag[...] * spot
-    k_up[1] = jnp.where(line == 0, 0.0, pltpu.roll(held, 1, 0))
-    k_down[1] = jnp.where(line == rows - 1, 0.0, pltpu.roll(held, rows - 1, 0))
+    def reach(mode):
+        spot = place[...]
+        held = stiff[...] * spot if mode else spot
+        scale = (lambda v: v) if mode else (lambda v: stiff[...] * v)
+        k_own[mode] = scale(sideways(held)) - diag[...] * spot
+        k_up[mode] = jnp.where(line == 0, 0.0, scale(pltpu.roll(held, 1, 0)))
+        k_down[mode] = jnp.where(line == rows - 1, 0.0, scale(pltpu.roll(held, rows - 1, 0)))
+
+    def force_panel():
+        at_row, _ = places()
+        at_h = iota(tall, 0) == at_row
+        mix = jnp.zeros(tall, F32)
+        for j in range(np_):
+            mix = jnp.where(at_h & (lane_node == j), to_col(extras[j, 2:3, 0:rows]), mix)
+        pan_force[0] = jnp.dot(mix, grown[...], precision=HIGH, preferred_element_type=F32)
 
     def send_round(mode, par, edges):
         resid = r[...]
@@ -317,14 +350,14 @@
         return coarse
 
     def side_row(mode, par, way):
-        pan_row = 2 * mode + (1 - way)
+        pan_row = 1 - way
         total = jnp.zeros((1, rows), F32)
         for j in range(np_):
-            total = total + info_in[way, pan_row : pan_row + 1, j * rows : (j + 1) * rows] * nbs[par, way, j, 0:1, :]
+            total = total + info_in[mode, way, pan_row : pan_row + 1, j * rows : (j + 1) * rows] * nbs[par, way, j, 0:1, :]
         value = jnp.sum(total, axis=1, keepdims=True)
         base = pieces * (1 - way)
         got = jnp.concatenate([rows_in[par, way, base + t : base + t + 1, :] for t in range(pieces)], axis=1)
-        return got + value * info_in[way, 4 + (1 - way) : 5 + (1 - way), 0:cols]
+        return got + value * info_in[mode, way, 2 + (1 - way) : 3 + (1 - way), 0:cols]
 
     def inner_resid(mode, base):
         v = z[...]
@@ -363,15 +396,39 @@
     def primal(k, carry):
         par = lax.rem(k, 2)
         send_round(0, par, True)
+
+        @pl.when(k == 0)
+        def _():
+            expand_sides(0)
+            reach(0)
+            epk[0:1, :] = to_row(stiff[:, 0:1])
+            epk[1:2, :] = to_row(stiff[:, cols - 1 : cols])
+            epk[2:3, :] = to_row(jnp.sum(place[...] * cm[...], axis=1, keepdims=True))
+            to_plates(epk, extras.at[b], x_send, x_recv)
+            extras[b] = epk[...]
+
+        @pl.when(k == 1)
+        def _():
+            wait_bytes(extras.at[pl.ds(0, np_ - 1)], x_recv)
+            wait_bytes(extras.at[pl.ds(0, np_ - 1)], x_send)
+            force_panel()
+            expand_columns(1)
+            expand_own(1)
+
+        @pl.when(k == 2)
+        def _():
+            expand_sides(1)
+            reach(1)
+
+        @pl.when(k == 3)
+        def _():
+            tt_hi[...], tt_lo[...] = split(tile[...].T)
+
         inner_resid(0, load)
 
         @pl.when(k == 0)
         def _():
-            for way in range(2):
-                @pl.when(has[way])
-                def _():
-                    wait_bytes(info_in.at[way], i_recv.at[way])
-                    wait_bytes(info_out, i_send.at[way])
+            wait_info(0)
 
         wait_round(par, True)
         outer_resid(0, par, finish(0, par))
@@ -380,26 +437,27 @@
     lax.fori_loop(0, ITERS - 1, primal, 0)
     par = (ITERS - 1) % 2
     send_round(0, par, False)
-    wait_round(par, False)
-    finish(0, par)
-    found[...] = x[...]
-    give_disp = pltpu.make_async_copy(found, out_disp, out_sem.at[0])
-    give_disp.start()
-
-    apk[...] = jnp.zeros(apk.shape, F32)
-    apk[0, 0:1, :] = to_row(jnp.sum(cm[...] * x[...], axis=1, keepdims=True))
+    apk[0, 0:1, :] = to_row(jnp.sum(cm[...] * z[...], axis=1, keepdims=True))
     to_plates(apk.at[0], fslots.at[b], a_send.at[0], a_recv.at[0])
     fslots[b] = apk[0]
+    wait_info(1)
+    wait_round(par, False)
     wait_bytes(fslots.at[pl.ds(0, np_ - 1)], a_recv.at[0])
     wait_bytes(fslots.at[pl.ds(0, np_ - 1)], a_send.at[0])
+
     force = fslots[0, 0:1, :]
     for j in range(1, np_):
         force = force + fslots[j, 0:1, :]
+    force = to_row(applied(pan_force, 0, par, eye * force))
     force = force * (8.0 / math.sqrt(cols * np_ * rows * ns))
     apk[1, 0:1, :] = force
     for d in range(1, ns):
         push(apk.at[1], tslots.at[s], a_send.at[1], a_recv.at[1], ((s + d) % ns, b))
     tslots[s] = apk[1]
+    finish(0, par)
+    found[...] = x[...]
+    give_disp = pltpu.make_async_copy(found, out_disp, out_sem.at[0])
+    give_disp.start()
     wait_bytes(tslots.at[pl.ds(0, ns - 1)], a_recv.at[1])
     wait_bytes(tslots.at[pl.ds(0, ns - 1)], a_send.at[1])
     over = jnp.zeros((1, rows), F32)
@@ -468,10 +526,15 @@
 
 
 def deliver(*refs):
-    copies = [pltpu.make_async_copy(refs[i], refs[4 + i], refs[8].at[i]) for i in range(4)]
-    for copy in copies:
+    source, target, room, sems = refs[:4], refs[4:8], refs[8:12], refs[12]
+    ins = [pltpu.make_async_copy(source[i], room[i], sems.at[0, i]) for i in range(4)]
+    outs = [pltpu.make_async_copy(room[i], target[i], sems.at[1, i]) for i in range(4)]
+    for copy in ins:
         copy.start()
-    for copy in copies:
+    for i in range(4):
+        ins[i].wait()
+        outs[i].start()
+    for copy in outs:
         copy.wait()
 
 
@@ -511,12 +574,19 @@
         + [square] * 4
         + [grown] * 3
         + [
-            pltpu.VMEM((8, wide), F32),
+            pltpu.VMEM((1, rows, np_ * rows), F32),
+            pltpu.VMEM((order, np_ * rows), F32),
+            pltpu.VMEM((order, order), F32),
             pltpu.VMEM((2, 8, wide), F32),
+            pltpu.VMEM((2, 2, 8, wide), F32),
             pltpu.VMEM((8, width), F32),
             pltpu.VMEM((np_, 8, width), F32),
             pltpu.VMEM((2, 8, width), F32),
             pltpu.VMEM((np_, order, order), F32),
+            pltpu.VMEM((8, LANES), F32),
+            pltpu.VMEM((np_, 8, LANES), F32),
+            dma,
+            dma,
             pltpu.VMEM((2, 8, LANES), F32),
             pltpu.VMEM((2, 8, LANES), F32),
             pltpu.VMEM((2, 8, LANES), F32),
@@ -529,7 +599,7 @@
             pltpu.VMEM((ns, 8, LANES), F32),
             pltpu.VMEM((np_, 8, LANES), F32),
             pltpu.VMEM((count, LANES), F32),
-            dma, dma, dma((2,)), dma((2,)), dma, dma, dma((2,)), dma((2,)),
+            dma, dma, dma((2,)), dma((2,)), dma, dma, dma((2, 2)), dma((2, 2)),
             dma((2,)), dma((2,)), *[dma((2, 2))] * 6, dma((3,)), dma((3,)),
         ],
         compiler_params=pltpu.CompilerParams(
@@ -541,7 +611,7 @@
         out_shape=tuple(jax.ShapeDtypeStruct(shape, F32) for shape in shapes),
         in_specs=[hbm] * 4,
         out_specs=(hbm,) * 4,
-        scratch_shapes=[dma((4,))],
+        scratch_shapes=[pltpu.VMEM(shape, F32) for shape in shapes] + [dma((2, 4))],
         compiler_params=pltpu.CompilerParams(vmem_limit_bytes=FULL),
     )(new_disp, adj, shear.reshape(rows), grads.reshape(count))
 

time: 92.2 us -> 72.3 us (0.78)
  Pallas kernels: 90.7 us -> 70.9 us
    pallas_call x1, Pallas kernels: 17.1 us -> 1.81 us  [on_device(): pl.pallas_call(deliver, out_shape=tuple((jax.ShapeDtypeStruct(shape, F32)...]
    pallas_call x1, Pallas kernels: 73.7 us -> 69.1 us  [on_device(): pl.pallas_call(functools.partial(kernel, ns, np_), out_shape=(jax.ShapeDt...]
where the time goes in v3:
time: 72.3 us; the launch traced here: 72.2 us
  Pallas kernels  70.9 us (98%)
  between operations  1.29 us (2%)
    pallas_call x1, Pallas kernels, on_device(): pl.pallas_call(functools.partial(kernel, ns, np_), out_shape=(jax.ShapeDt...  69.1 us
    pallas_call x1, Pallas kernels, on_device(): pl.pallas_call(deliver, out_shape=tuple((jax.ShapeDtypeStruct(shape, F32)...  1.81 us

profile of v3, /device:TPU:0, one launch (start us, length us, event | category | flops | bytes accessed | tf_op | source)
XLA Modules:
  0.0 72.2 jit_solution(9126507317934216568)
XLA Ops:
  1.3 69.1 %shard_map.138 = (f32[128,512]{1,0:T(8,128)}, f32[128,512]{1,0:T(8,128)}, f32[1,128]{1,0:T(1,128)}, f32[1,64]{1,0:T(1,128)}) custom-call(f32[128,512]{1,0:T(8,128)} %load_in.1, f32[128,512]{1,0:T(8,128)} %disp_in.1, f32[128,512]{1,0:T(8,128)} %mass_in.1, s32[128,512]{1,0:T(8,128)} %wall_in.1, f32[4]{0:T(128)} %cstiff.1, s32[128,512]{1,0:T(8,128)} %dmap_in.1, ...), custom_call_target="tpu_custom_call" | custom-call | tf_op jit(solution)/shard_map/pallas_call | solution.py:559
  70.3 1.8 %shard_map.139 = (f32[128,512]{1,0:T(8,128)}, f32[128,512]{1,0:T(8,128)}, f32[128]{0:T(128)}, f32[64]{0:T(128)}) custom-call(f32[128,512]{1,0:T(8,128)} %get-tuple-element.8.refs_0_, f32[128,512]{1,0:T(8,128)} %get-tuple-element.9.refs_1_, f32[128]{0:T(128)} %bitcast.2, f32[64]{0:T(128)} %bitcast.3), custom_call_target="tpu_custom_call" | custom-call | tf_op jit(solution)/shard_map/pallas_call | solution.py:609

commit v4 on v3

--- a/solution.py
+++ b/solution.py
@@ -53,10 +53,10 @@
     t_hi, t_lo, tt_hi, tt_lo,
     pan_own, pan_left, pan_right, pan_force, grown, used, info_out, info_in,
     spk, sslots, snb, pslots, epk, extras, x_send, x_recv,
-    gpk, cpk, rpk, slots, nbs, cols_in, rows_in,
+    gpk, rpk, slots, nbs, rows_in, edge_tile,
     apk, fslots, tslots, gslots, seg,
     s_send, s_recv, n_send, n_recv, p_send, p_recv, i_send, i_recv,
-    r_send, r_recv, rn_send, rn_recv, c_send, c_recv, e_send, e_recv, a_send, a_recv,
+    r_send, r_recv, rn_send, rn_recv, e_send, e_recv, a_send, a_recv,
 ):
     rows, cols = load.shape
     nodes = nidx.shape[1]
@@ -68,6 +68,10 @@
     b = lax.axis_index("plate")
     has = (s > 0, s < ns - 1)
     beside = (s - 1, s + 1)
+    miss = (1 - jnp.minimum(s, 1), 1 - jnp.minimum(ns - 1 - s, 1))
+    toward = (jnp.maximum(s - 1, 0), jnp.minimum(s + 1, ns - 1))
+    lands = tuple((1 - way) * (1 - miss[way]) + way * miss[way] for way in range(2))
+    same = tuple((b + miss[way]) % np_ for way in range(2))
 
     ways = ((disp_in, disp), (wall_in, wall), (mass_in, mass), (dmap_in, dmap), (tile_in, tile), (load_in, load))
     loads = [pltpu.make_async_copy(src, dst, in_sem.at[i]) for i, (src, dst) in enumerate(ways)]
@@ -108,8 +112,6 @@
     spk[3:4, 0:rows] = to_row(disp[:, 0:1])
     spk[4:5, 0:rows] = to_row(disp[:, cols - 1 : cols])
     to_plates(spk, sslots.at[b], s_send, s_recv)
-    flank = (b > 0, b < np_ - 1)
-    flanking = (b - 1, b + 1)
     for way in range(2):
         @pl.when(has[way])
         def _():
@@ -120,13 +122,6 @@
             snb[way] = jnp.zeros(snb.shape[1:], F32)
             for i in range(2):
                 info_in[i, way] = jnp.zeros(info_in.shape[2:], F32)
-                nbs[i, way] = jnp.zeros(nbs.shape[2:], F32)
-                rows_in[i, way] = jnp.zeros(rows_in.shape[2:], F32)
-
-        @pl.when(jnp.logical_not(flank[way]))
-        def _():
-            for i in range(2):
-                cols_in[i, way] = jnp.zeros(cols_in.shape[2:], F32)
 
     loads[1].wait()
     level = jnp.zeros((rows, cols), F32)
@@ -151,6 +146,9 @@
     lax.fori_loop(0, rows // 8, lookup, 0)
     loads[4].wait()
     t_hi[...], t_lo[...] = split(tile[...])
+    for i, at in enumerate((0, cols - 1)):
+        edge_tile[0, i : i + 1, :] = to_row(tile[:, at : at + 1])
+        edge_tile[1, i : i + 1, :] = tile[at : at + 1, :]
 
     loads[5].wait()
     loads[6].wait()
@@ -277,63 +275,46 @@
 
     def send_round(mode, par, edges):
         resid = r[...]
+        scaled = resid * rdiag[...]
         gpk[par, 0:1, :] = to_row(jnp.sum(resid * place[...], axis=1, keepdims=True))
+        if edges:
+            for i, at in enumerate((0, cols - 1)):
+                value = x[:, at : at + 1] + jnp.sum(scaled * edge_tile[mode, i : i + 1, :], axis=1, keepdims=True)
+                gpk[par, 1 + i : 2 + i, :] = to_row(value * stiff[:, at : at + 1] if mode else value)
         for way in range(2):
-            @pl.when(has[way])
-            def _():
-                for d in range(np_):
-                    push(
-                        gpk.at[par], nbs.at[par, 1 - way, b], rn_send.at[par, way],
-                        rn_recv.at[par, 1 - way], (beside[way], (b + d) % np_),
-                    )
+            for d in range(np_):
+                if d:
+                    plate, slot = (b + d) % np_, b
+                else:
+                    plate, slot = same[way], same[way]
+                push(gpk.at[par], nbs.at[par, lands[way], slot], rn_send.at[par], rn_recv.at[par], (toward[way], plate))
         to_plates(gpk.at[par], slots.at[par, b], r_send.at[par], r_recv.at[par])
         slots[par, b] = gpk[par]
-        hi, lo = split(resid * rdiag[...])
+        hi, lo = split(scaled)
         wh, wl = (tt_hi, tt_lo) if mode else (t_hi, t_lo)
         both = jnp.dot(jnp.concatenate([hi, lo], axis=0), wh[...], preferred_element_type=F32)
         band = both[:rows] + both[rows:] + jnp.dot(hi, wl[...], preferred_element_type=F32)
-        z[...] = x[...] + band
+        total = x[...] + band
+        z[...] = total
         if not edges:
             return
-        edge = (lambda *at: z[at] * stiff[at]) if mode else (lambda *at: z[at])
-        first, last = edge(slice(0, 1), slice(None)), edge(slice(rows - 1, rows), slice(None))
+        first, last = total[0:1, :], total[rows - 1 : rows, :]
+        if mode:
+            first, last = first * stiff[0:1, :], last * stiff[rows - 1 : rows, :]
         for t in range(pieces):
             rpk[par, t : t + 1, :] = first[:, t * LANES : (t + 1) * LANES]
             rpk[par, pieces + t : pieces + t + 1, :] = last[:, t * LANES : (t + 1) * LANES]
         for way in range(2):
-            @pl.when(has[way])
-            def _():
-                push(
-                    rpk.at[par], rows_in.at[par, 1 - way], e_send.at[par, way],
-                    e_recv.at[par, 1 - way], (beside[way], b),
-                )
-        cpk[par, 0:1, :] = to_row(edge(slice(None), slice(0, 1)))
-        cpk[par, 1:2, :] = to_row(edge(slice(None), slice(cols - 1, cols)))
-        for side in range(2):
-            @pl.when(flank[side])
-            def _():
-                push(
-                    cpk.at[par], cols_in.at[par, 1 - side], c_send.at[par, side],
-                    c_recv.at[par, 1 - side], (s, flanking[side]),
-                )
+            push(rpk.at[par], rows_in.at[par, lands[way]], e_send.at[par], e_recv.at[par], (toward[way], same[way]))
 
     def wait_round(par, edges):
         wait_bytes(slots.at[par, pl.ds(0, np_ - 1)], r_recv.at[par])
+        wait_bytes(nbs.at[par], rn_recv.at[par])
+        if edges:
+            wait_bytes(rows_in.at[par], e_recv.at[par])
+            wait_bytes(rows_in.at[par], e_send.at[par])
         wait_bytes(slots.at[par, pl.ds(0, np_ - 1)], r_send.at[par])
-        for way in range(2):
-            @pl.when(has[way])
-            def _():
-                wait_bytes(nbs.at[par, way], rn_recv.at[par, way])
-                wait_bytes(nbs.at[par, way], rn_send.at[par, way])
-                if edges:
-                    wait_bytes(rpk.at[par], e_recv.at[par, way])
-                    wait_bytes(rpk.at[par], e_send.at[par, way])
-        if edges:
-            for side in range(2):
-                @pl.when(flank[side])
-                def _():
-                    wait_bytes(cpk.at[par], c_recv.at[par, side])
-                    wait_bytes(cpk.at[par], c_send.at[par, side])
+        wait_bytes(nbs.at[par], rn_send.at[par])
 
     def applied(mat, mode, par, extra=None):
         total = extra
@@ -357,6 +338,7 @@
         value = jnp.sum(total, axis=1, keepdims=True)
         base = pieces * (1 - way)
         got = jnp.concatenate([rows_in[par, way, base + t : base + t + 1, :] for t in range(pieces)], axis=1)
+        got = jnp.where(has[way], got, 0.0)
         return got + value * info_in[mode, way, 2 + (1 - way) : 3 + (1 - way), 0:cols]
 
     def inner_resid(mode, base):
@@ -369,8 +351,10 @@
 
     def outer_resid(mode, par, coarse):
         up, down = pltpu.roll(coarse, 1, 0), pltpu.roll(coarse, rows - 1, 0)
-        west = applied(pan_left, mode, par, eye * cols_in[par, 0, 1:2, :])
-        east = applied(pan_right, mode, par, eye * cols_in[par, 1, 0:1, :])
+        west = jnp.where(b > 0, slots[par, left_slot, 2:3, :], 0.0)
+        east = jnp.where(b < np_ - 1, slots[par, right_slot, 1:2, :], 0.0)
+        west = applied(pan_left, mode, par, eye * west)
+        east = applied(pan_right, mode, par, eye * east)
         thin = iota((rows, LANES), 1)
         for t in range(pieces):
             part = slice(t * LANES, (t + 1) * LANES)
@@ -489,17 +473,13 @@
 
     lax.fori_loop(0, ITERS - 1, adjoint, 0)
     send_round(1, par, False)
-    wait_round(par, False)
-    finish(1, par)
-    give_adj = pltpu.make_async_copy(x, out_adj, out_sem.at[1])
-    give_adj.start()
-
-    z[...] = x[...] * found[...]
+
+    q[...] = z[...] * found[...]
     group = 8
     for first in range(0, count, group):
         def gather(i, accs):
             part = pl.ds(pl.multiple_of(i * 8, 8), 8)
-            ids, vals = dmap[part, :], z[part, :]
+            ids, vals = dmap[part, :], q[part, :]
             res = []
             for d in range(group):
                 kept = jnp.where(ids == first + d, vals, 0.0)
@@ -512,7 +492,16 @@
         accs = lax.fori_loop(0, rows // 8, gather, tuple(jnp.zeros((8, LANES), F32) for _ in range(group)))
         for d in range(group):
             seg[first + d : first + d + 1, :] = jnp.sum(accs[d], axis=0, keepdims=True)
-    apk[2, 0:1, 0:count] = to_row(jnp.sum(seg[...], axis=1, keepdims=True))
+    sums = to_row(jnp.sum(seg[...], axis=1, keepdims=True))
+    damper = jnp.sum(place[...] * dmap[...].astype(F32), axis=1, keepdims=True)
+    held = jnp.sum(place[...] * found[...], axis=1, keepdims=True)
+    hits = jnp.where(damper == iota((rows, count), 1).astype(F32), held, 0.0)
+    wait_round(par, False)
+    coarse = finish(1, par)
+    give_adj = pltpu.make_async_copy(x, out_adj, out_sem.at[1])
+    give_adj.start()
+    sums = sums + jnp.sum(hits * coarse[:, 0:count], axis=0, keepdims=True)
+    apk[2, 0:1, 0:count] = sums
     to_plates(apk.at[2], gslots.at[b], a_send.at[2], a_recv.at[2])
     gslots[b] = apk[2]
     wait_bytes(gslots.at[pl.ds(0, np_ - 1)], a_recv.at[2])
@@ -589,18 +578,17 @@
             dma,
             pltpu.VMEM((2, 8, LANES), F32),
             pltpu.VMEM((2, 8, LANES), F32),
-            pltpu.VMEM((2, 8, LANES), F32),
             pltpu.VMEM((2, np_, 8, LANES), F32),
             pltpu.VMEM((2, 2, np_, 8, LANES), F32),
             pltpu.VMEM((2, 2, 8, LANES), F32),
-            pltpu.VMEM((2, 2, 8, LANES), F32),
+            pltpu.VMEM((2, 8, cols), F32),
             pltpu.VMEM((3, 8, LANES), F32),
             pltpu.VMEM((np_, 8, LANES), F32),
             pltpu.VMEM((ns, 8, LANES), F32),
             pltpu.VMEM((np_, 8, LANES), F32),
             pltpu.VMEM((count, LANES), F32),
             dma, dma, dma((2,)), dma((2,)), dma, dma, dma((2, 2)), dma((2, 2)),
-            dma((2,)), dma((2,)), *[dma((2, 2))] * 6, dma((3,)), dma((3,)),
+            *[dma((2,))] * 6, dma((3,)), dma((3,)),
         ],
         compiler_params=pltpu.CompilerParams(
             collective_id=0, has_side_effects=True, vmem_limit_bytes=FULL

time: 72.3 us -> 71.2 us (0.985)
  Pallas kernels: 70.9 us -> 69.7 us
    pallas_call x1, Pallas kernels: 69.1 us -> 67.9 us  [on_device(): pl.pallas_call(functools.partial(kernel, ns, np_), out_shape=(jax.ShapeDt...]
where the time goes in v4:
time: 71.2 us; the launch traced here: 71 us
  Pallas kernels  69.7 us (98%)
  between operations  1.29 us (2%)
    pallas_call x1, Pallas kernels, on_device(): pl.pallas_call(functools.partial(kernel, ns, np_), out_shape=(jax.ShapeDt...  67.9 us
    pallas_call x1, Pallas kernels, on_device(): pl.pallas_call(deliver, out_shape=tuple((jax.ShapeDtypeStruct(shape, F32)...  1.81 us

profile of v4, /device:TPU:0, one launch (start us, length us, event | category | flops | bytes accessed | tf_op | source)
XLA Modules:
  0.0 71.0 jit_solution(12355613728404551465)
XLA Ops:
  1.3 67.9 %shard_map.138 = (f32[128,512]{1,0:T(8,128)}, f32[128,512]{1,0:T(8,128)}, f32[1,128]{1,0:T(1,128)}, f32[1,64]{1,0:T(1,128)}) custom-call(f32[128,512]{1,0:T(8,128)} %load_in.1, f32[128,512]{1,0:T(8,128)} %disp_in.1, f32[128,512]{1,0:T(8,128)} %mass_in.1, s32[128,512]{1,0:T(8,128)} %wall_in.1, f32[4]{0:T(128)} %cstiff.1, s32[128,512]{1,0:T(8,128)} %dmap_in.1, ...), custom_call_target="tpu_custom_call" | custom-call | tf_op jit(solution)/shard_map/pallas_call | solution.py:548
  69.2 1.8 %shard_map.139 = (f32[128,512]{1,0:T(8,128)}, f32[128,512]{1,0:T(8,128)}, f32[128]{0:T(128)}, f32[64]{0:T(128)}) custom-call(f32[128,512]{1,0:T(8,128)} %get-tuple-element.8.refs_0_, f32[128,512]{1,0:T(8,128)} %get-tuple-element.9.refs_1_, f32[128]{0:T(128)} %bitcast.2, f32[64]{0:T(128)} %bitcast.3), custom_call_target="tpu_custom_call" | custom-call | tf_op jit(solution)/shard_map/pallas_call | solution.py:597

commit v5 on v4

--- a/solution.py
+++ b/solution.py
@@ -53,7 +53,7 @@
     t_hi, t_lo, tt_hi, tt_lo,
     pan_own, pan_left, pan_right, pan_force, grown, used, info_out, info_in,
     spk, sslots, snb, pslots, epk, extras, x_send, x_recv,
-    gpk, rpk, slots, nbs, rows_in, edge_tile,
+    g1, gpk, rpk, slots, nbs, rows_in, edge_tile,
     apk, fslots, tslots, gslots, seg,
     s_send, s_recv, n_send, n_recv, p_send, p_recv, i_send, i_recv,
     r_send, r_recv, rn_send, rn_recv, e_send, e_recv, a_send, a_recv,
@@ -276,7 +276,8 @@
     def send_round(mode, par, edges):
         resid = r[...]
         scaled = resid * rdiag[...]
-        gpk[par, 0:1, :] = to_row(jnp.sum(resid * place[...], axis=1, keepdims=True))
+        g1[par] = to_row(jnp.sum(resid * place[...], axis=1, keepdims=True))
+        gpk[par, 0:1, :] = g1[par]
         if edges:
             for i, at in enumerate((0, cols - 1)):
                 value = x[:, at : at + 1] + jnp.sum(scaled * edge_tile[mode, i : i + 1, :], axis=1, keepdims=True)
@@ -287,7 +288,7 @@
                     plate, slot = (b + d) % np_, b
                 else:
                     plate, slot = same[way], same[way]
-                push(gpk.at[par], nbs.at[par, lands[way], slot], rn_send.at[par], rn_recv.at[par], (toward[way], plate))
+                push(g1.at[par], nbs.at[par, lands[way], slot], rn_send.at[par], rn_recv.at[par], (toward[way], plate))
         to_plates(gpk.at[par], slots.at[par, b], r_send.at[par], r_recv.at[par])
         slots[par, b] = gpk[par]
         hi, lo = split(scaled)
@@ -302,10 +303,10 @@
         if mode:
             first, last = first * stiff[0:1, :], last * stiff[rows - 1 : rows, :]
         for t in range(pieces):
-            rpk[par, t : t + 1, :] = first[:, t * LANES : (t + 1) * LANES]
-            rpk[par, pieces + t : pieces + t + 1, :] = last[:, t * LANES : (t + 1) * LANES]
+            rpk[par, 0, t : t + 1, :] = first[:, t * LANES : (t + 1) * LANES]
+            rpk[par, 1, t : t + 1, :] = last[:, t * LANES : (t + 1) * LANES]
         for way in range(2):
-            push(rpk.at[par], rows_in.at[par, lands[way]], e_send.at[par], e_recv.at[par], (toward[way], same[way]))
+            push(rpk.at[par, way], rows_in.at[par, lands[way]], e_send.at[par], e_recv.at[par], (toward[way], same[way]))
 
     def wait_round(par, edges):
         wait_bytes(slots.at[par, pl.ds(0, np_ - 1)], r_recv.at[par])
@@ -336,8 +337,7 @@
         for j in range(np_):
             total = total + info_in[mode, way, pan_row : pan_row + 1, j * rows : (j + 1) * rows] * nbs[par, way, j, 0:1, :]
         value = jnp.sum(total, axis=1, keepdims=True)
-        base = pieces * (1 - way)
-        got = jnp.concatenate([rows_in[par, way, base + t : base + t + 1, :] for t in range(pieces)], axis=1)
+        got = jnp.concatenate([rows_in[par, way, t : t + 1, :] for t in range(pieces)], axis=1)
         got = jnp.where(has[way], got, 0.0)
         return got + value * info_in[mode, way, 2 + (1 - way) : 3 + (1 - way), 0:cols]
 
@@ -576,16 +576,17 @@
             pltpu.VMEM((np_, 8, LANES), F32),
             dma,
             dma,
-            pltpu.VMEM((2, 8, LANES), F32),
-            pltpu.VMEM((2, 8, LANES), F32),
-            pltpu.VMEM((2, np_, 8, LANES), F32),
-            pltpu.VMEM((2, 2, np_, 8, LANES), F32),
-            pltpu.VMEM((2, 2, 8, LANES), F32),
+            pltpu.VMEM((2, 1, LANES), F32),
+            pltpu.VMEM((2, 4, LANES), F32),
+            pltpu.VMEM((2, 2, cols // LANES, LANES), F32),
+            pltpu.VMEM((2, np_, 4, LANES), F32),
+            pltpu.VMEM((2, 2, np_, 1, LANES), F32),
+            pltpu.VMEM((2, 2, cols // LANES, LANES), F32),
             pltpu.VMEM((2, 8, cols), F32),
-            pltpu.VMEM((3, 8, LANES), F32),
-            pltpu.VMEM((np_, 8, LANES), F32),
-            pltpu.VMEM((ns, 8, LANES), F32),
-            pltpu.VMEM((np_, 8, LANES), F32),
+            pltpu.VMEM((3, 1, LANES), F32),
+            pltpu.VMEM((np_, 1, LANES), F32),
+            pltpu.VMEM((ns, 1, LANES), F32),
+            pltpu.VMEM((np_, 1, LANES), F32),
             pltpu.VMEM((count, LANES), F32),
             dma, dma, dma((2,)), dma((2,)), dma, dma, dma((2, 2)), dma((2, 2)),
             *[dma((2,))] * 6, dma((3,)), dma((3,)),

time: 71.2 us -> 69.7 us (0.979)
  Pallas kernels: 69.7 us -> 68.2 us
    pallas_call x1, Pallas kernels: 67.9 us -> 66.4 us  [on_device(): pl.pallas_call(functools.partial(kernel, ns, np_), out_shape=(jax.ShapeDt...]
where the time goes in v5:
time: 69.7 us; the launch traced here: 69.5 us
  Pallas kernels  68.2 us (98%)
  between operations  1.29 us (2%)
    pallas_call x1, Pallas kernels, on_device(): pl.pallas_call(functools.partial(kernel, ns, np_), out_shape=(jax.ShapeDt...  66.4 us
    pallas_call x1, Pallas kernels, on_device(): pl.pallas_call(deliver, out_shape=tuple((jax.ShapeDtypeStruct(shape, F32)...  1.81 us

profile of v5, /device:TPU:0, one launch (start us, length us, event | category | flops | bytes accessed | tf_op | source)
XLA Modules:
  0.0 69.5 jit_solution(9872750327347381369)
XLA Ops:
  1.3 66.4 %shard_map.138 = (f32[128,512]{1,0:T(8,128)}, f32[128,512]{1,0:T(8,128)}, f32[1,128]{1,0:T(1,128)}, f32[1,64]{1,0:T(1,128)}) custom-call(f32[128,512]{1,0:T(8,128)} %load_in.1, f32[128,512]{1,0:T(8,128)} %disp_in.1, f32[128,512]{1,0:T(8,128)} %mass_in.1, s32[128,512]{1,0:T(8,128)} %wall_in.1, f32[4]{0:T(128)} %cstiff.1, s32[128,512]{1,0:T(8,128)} %dmap_in.1, ...), custom_call_target="tpu_custom_call" | custom-call | tf_op jit(solution)/shard_map/pallas_call | solution.py:548
  67.7 1.8 %shard_map.139 = (f32[128,512]{1,0:T(8,128)}, f32[128,512]{1,0:T(8,128)}, f32[128]{0:T(128)}, f32[64]{0:T(128)}) custom-call(f32[128,512]{1,0:T(8,128)} %get-tuple-element.8.refs_0_, f32[128,512]{1,0:T(8,128)} %get-tuple-element.9.refs_1_, f32[128]{0:T(128)} %bitcast.2, f32[64]{0:T(128)} %bitcast.3), custom_call_target="tpu_custom_call" | custom-call | tf_op jit(solution)/shard_map/pallas_call | solution.py:598

commit v6 on v5

--- a/solution.py
+++ b/solution.py
@@ -308,8 +308,10 @@
         for way in range(2):
             push(rpk.at[par, way], rows_in.at[par, lands[way]], e_send.at[par], e_recv.at[par], (toward[way], same[way]))
 
-    def wait_round(par, edges):
+    def wait_plates(par):
         wait_bytes(slots.at[par, pl.ds(0, np_ - 1)], r_recv.at[par])
+
+    def wait_storeys(par, edges):
         wait_bytes(nbs.at[par], rn_recv.at[par])
         if edges:
             wait_bytes(rows_in.at[par], e_recv.at[par])
@@ -365,6 +367,8 @@
             if t == pieces - 1:
                 total = total + jnp.where(thin == LANES - 1, east if mode else east * stiff[:, part], 0.0)
             r[:, part] = total
+
+    def edge_resid(mode, par):
         top, bottom = side_row(mode, par, 0), side_row(mode, par, 1)
         if mode == 0:
             top, bottom = top * stiff[0:1, :], bottom * stiff[rows - 1 : rows, :]
@@ -409,13 +413,15 @@
             tt_hi[...], tt_lo[...] = split(tile[...].T)
 
         inner_resid(0, load)
+        wait_plates(par)
 
         @pl.when(k == 0)
         def _():
             wait_info(0)
 
-        wait_round(par, True)
         outer_resid(0, par, finish(0, par))
+        wait_storeys(par, True)
+        edge_resid(0, par)
         return carry
 
     lax.fori_loop(0, ITERS - 1, primal, 0)
@@ -425,7 +431,7 @@
     to_plates(apk.at[0], fslots.at[b], a_send.at[0], a_recv.at[0])
     fslots[b] = apk[0]
     wait_info(1)
-    wait_round(par, False)
+    wait_plates(par)
     wait_bytes(fslots.at[pl.ds(0, np_ - 1)], a_recv.at[0])
     wait_bytes(fslots.at[pl.ds(0, np_ - 1)], a_send.at[0])
 
@@ -438,6 +444,7 @@
     for d in range(1, ns):
         push(apk.at[1], tslots.at[s], a_send.at[1], a_recv.at[1], ((s + d) % ns, b))
     tslots[s] = apk[1]
+    wait_storeys(par, False)
     finish(0, par)
     found[...] = x[...]
     give_disp = pltpu.make_async_copy(found, out_disp, out_sem.at[0])
@@ -467,8 +474,10 @@
         par = lax.rem(k, 2)
         send_round(1, par, True)
         inner_resid(1, q)
-        wait_round(par, True)
+        wait_plates(par)
         outer_resid(1, par, finish(1, par))
+        wait_storeys(par, True)
+        edge_resid(1, par)
         return carry
 
     lax.fori_loop(0, ITERS - 1, adjoint, 0)
@@ -496,7 +505,7 @@
     damper = jnp.sum(place[...] * dmap[...].astype(F32), axis=1, keepdims=True)
     held = jnp.sum(place[...] * found[...], axis=1, keepdims=True)
     hits = jnp.where(damper == iota((rows, count), 1).astype(F32), held, 0.0)
-    wait_round(par, False)
+    wait_plates(par)
     coarse = finish(1, par)
     give_adj = pltpu.make_async_copy(x, out_adj, out_sem.at[1])
     give_adj.start()
@@ -504,6 +513,7 @@
     apk[2, 0:1, 0:count] = sums
     to_plates(apk.at[2], gslots.at[b], a_send.at[2], a_recv.at[2])
     gslots[b] = apk[2]
+    wait_storeys(par, False)
     wait_bytes(gslots.at[pl.ds(0, np_ - 1)], a_recv.at[2])
     wait_bytes(gslots.at[pl.ds(0, np_ - 1)], a_send.at[2])
     sums = gslots[0, 0:1, 0:count]

time: 69.7 us -> 68.2 us (0.978)
  Pallas kernels: 68.2 us -> 66.8 us
    pallas_call x1, Pallas kernels: 66.4 us -> 65 us  [on_device(): pl.pallas_call(functools.partial(kernel, ns, np_), out_shape=(jax.ShapeDt...]
where the time goes in v6:
time: 68.2 us; the launch traced here: 68.1 us
  Pallas kernels  66.8 us (98%)
  between operations  1.29 us (2%)
    pallas_call x1, Pallas kernels, on_device(): pl.pallas_call(functools.partial(kernel, ns, np_), out_shape=(jax.ShapeDt...  65 us
    pallas_call x1, Pallas kernels, on_device(): pl.pallas_call(deliver, out_shape=tuple((jax.ShapeDtypeStruct(shape, F32)...  1.81 us

profile of v6, /device:TPU:0, one launch (start us, length us, event | category | flops | bytes accessed | tf_op | source)
XLA Modules:
  0.0 68.1 jit_solution(16547617179453366160)
XLA Ops:
  1.3 65.0 %shard_map.138 = (f32[128,512]{1,0:T(8,128)}, f32[128,512]{1,0:T(8,128)}, f32[1,128]{1,0:T(1,128)}, f32[1,64]{1,0:T(1,128)}) custom-call(f32[128,512]{1,0:T(8,128)} %load_in.1, f32[128,512]{1,0:T(8,128)} %disp_in.1, f32[128,512]{1,0:T(8,128)} %mass_in.1, s32[128,512]{1,0:T(8,128)} %wall_in.1, f32[4]{0:T(128)} %cstiff.1, s32[128,512]{1,0:T(8,128)} %dmap_in.1, ...), custom_call_target="tpu_custom_call" | custom-call | tf_op jit(solution)/shard_map/pallas_call | solution.py:558
  66.3 1.8 %shard_map.139 = (f32[128,512]{1,0:T(8,128)}, f32[128,512]{1,0:T(8,128)}, f32[128]{0:T(128)}, f32[64]{0:T(128)}) custom-call(f32[128,512]{1,0:T(8,128)} %get-tuple-element.8.refs_0_, f32[128,512]{1,0:T(8,128)} %get-tuple-element.9.refs_1_, f32[128]{0:T(128)} %bitcast.2, f32[64]{0:T(128)} %bitcast.3), custom_call_target="tpu_custom_call" | custom-call | tf_op jit(solution)/shard_map/pallas_call | solution.py:608

commit v7 on v6

--- a/solution.py
+++ b/solution.py
@@ -282,6 +282,7 @@
             for i, at in enumerate((0, cols - 1)):
                 value = x[:, at : at + 1] + jnp.sum(scaled * edge_tile[mode, i : i + 1, :], axis=1, keepdims=True)
                 gpk[par, 1 + i : 2 + i, :] = to_row(value * stiff[:, at : at + 1] if mode else value)
+        to_plates(gpk.at[par], slots.at[par, b], r_send.at[par], r_recv.at[par])
         for way in range(2):
             for d in range(np_):
                 if d:
@@ -289,7 +290,6 @@
                 else:
                     plate, slot = same[way], same[way]
                 push(g1.at[par], nbs.at[par, lands[way], slot], rn_send.at[par], rn_recv.at[par], (toward[way], plate))
-        to_plates(gpk.at[par], slots.at[par, b], r_send.at[par], r_recv.at[par])
         slots[par, b] = gpk[par]
         hi, lo = split(scaled)
         wh, wl = (tt_hi, tt_lo) if mode else (t_hi, t_lo)

time: 68.2 us -> 68.3 us (level)
  no operation moved by 1% of the time
where the time goes in v7:
time: 68.3 us; the launch traced here: 68.2 us
  Pallas kernels  66.9 us (98%)
  between operations  1.29 us (2%)
    pallas_call x1, Pallas kernels, on_device(): pl.pallas_call(functools.partial(kernel, ns, np_), out_shape=(jax.ShapeDt...  65 us
    pallas_call x1, Pallas kernels, on_device(): pl.pallas_call(deliver, out_shape=tuple((jax.ShapeDtypeStruct(shape, F32)...  1.81 us

profile of v7, /device:TPU:0, one launch (start us, length us, event | category | flops | bytes accessed | tf_op | source)
XLA Modules:
  0.0 68.2 jit_solution(14356424878771686882)
XLA Ops:
  1.3 65.0 %shard_map.138 = (f32[128,512]{1,0:T(8,128)}, f32[128,512]{1,0:T(8,128)}, f32[1,128]{1,0:T(1,128)}, f32[1,64]{1,0:T(1,128)}) custom-call(f32[128,512]{1,0:T(8,128)} %load_in.1, f32[128,512]{1,0:T(8,128)} %disp_in.1, f32[128,512]{1,0:T(8,128)} %mass_in.1, s32[128,512]{1,0:T(8,128)} %wall_in.1, f32[4]{0:T(128)} %cstiff.1, s32[128,512]{1,0:T(8,128)} %dmap_in.1, ...), custom_call_target="tpu_custom_call" | custom-call | tf_op jit(solution)/shard_map/pallas_call | solution.py:558
  66.3 1.8 %shard_map.139 = (f32[128,512]{1,0:T(8,128)}, f32[128,512]{1,0:T(8,128)}, f32[128]{0:T(128)}, f32[64]{0:T(128)}) custom-call(f32[128,512]{1,0:T(8,128)} %get-tuple-element.8.refs_0_, f32[128,512]{1,0:T(8,128)} %get-tuple-element.9.refs_1_, f32[128]{0:T(128)} %bitcast.2, f32[64]{0:T(128)} %bitcast.3), custom_call_target="tpu_custom_call" | custom-call | tf_op jit(solution)/shard_map/pallas_call | solution.py:608
